TPU v7x, 512 devices: a whole 4x8x8 slice. The times are simulated.
512 devices in a mesh: gx: 8 (over y_lo, core), gy: 8 (over x, y_hi), gz: 8 (over z).
Axes of the slice: x: 4, y: 8 (y_hi: 2, y_lo: 4; y = y_hi * 4 + y_lo), z: 8, core: 2. Of those that a mesh axis runs over, the one named last changes fastest.
Arguments:
- inputs: bfloat16 [448, 12288], P(('gx', 'gz'), 'gy'), may hold values from -6 to 6
- weight_in: bfloat16 [12288, 24576], P('gy', ('gx', 'gz')), may hold values from -0.0546875 to 0.0546875
- weight_out: bfloat16 [24576, 12288], P(('gx', 'gz'), 'gy'), may hold values from -0.0390625 to 0.0390625
- grad_output: bfloat16 [448, 12288], P(('gx', 'gz'), 'gy'), may hold values from -6 to 6
Outputs:
- grad_inputs: bfloat16 [448, 12288], P(('gx', 'gz'), 'gy')
- grad_weight_in: bfloat16 [12288, 24576], P('gy', ('gx', 'gz'))
- grad_weight_out: bfloat16 [24576, 12288], P(('gx', 'gz'), 'gy')
All inputs are finite; a program needn't handle non-finite values.
Results may differ from a plain program's by a relative error of at most 0.0049.
Values may be sent and summed in bfloat16 or wider, within the bound.
No kernel may reach another device: no remote copies, remote signals or barrier semaphores. Data moves between devices by JAX's collectives and lax.ppermute only.
A program may use at most 64 MiB of HBM per device.

v0:
```python
import jax
import jax.numpy as jnp
from jax import lax
from jax.sharding import PartitionSpec as P

coeff = 0.7978845608


def gelu_value(v):
    inner = jnp.tanh(coeff * (v + 0.044715 * v * v * v))
    return 0.5 * v * (1.0 + inner)


def gelu_slope(v):
    inner = jnp.tanh(coeff * (v + 0.044715 * v * v * v))
    return 0.5 * (1.0 + inner) + 0.5 * v * (1.0 - inner * inner) * coeff * (1.0 + 0.134145 * v * v)


def contract_last(left, right):
    return lax.dot_general(
        left, right, (((1,), (1,)), ((), ())), preferred_element_type=jnp.float32
    )


def contract_first(left, right):
    return lax.dot_general(
        left, right, (((0,), (0,)), ((), ())), preferred_element_type=jnp.float32
    )


def per_device(inputs, weight_in, weight_out, grad_output):
    gathered_in, gathered_grad = (
        lax.all_gather(inputs, ("gx", "gz"), axis=0, tiled=True),
        lax.all_gather(grad_output, ("gx", "gz"), axis=0, tiled=True),
    )
    pre_part = jnp.dot(gathered_in, weight_in, preferred_element_type=jnp.float32)
    dact_part = contract_last(gathered_grad, weight_out)
    total_rows = gathered_in.shape[0]
    share_rows = total_rows // lax.axis_size("gy")
    pre_whole = lax.psum(pre_part, "gy")
    activated = gelu_value(pre_whole).astype(jnp.bfloat16)
    dact_own = lax.psum_scatter(dact_part, "gy", scatter_dimension=0, tiled=True)
    first_row = lax.axis_index("gy") * share_rows
    pre_own = lax.dynamic_slice_in_dim(pre_whole, first_row, share_rows, 0)
    dpre_own = (dact_own * gelu_slope(pre_own)).astype(jnp.bfloat16)
    dpre_all = lax.all_gather(dpre_own, "gy", axis=0, tiled=True)
    grad_weight_out = contract_first(activated, gathered_grad).astype(jnp.bfloat16)
    grad_weight_in = contract_first(gathered_in, dpre_all).astype(jnp.bfloat16)
    grad_inputs = lax.psum_scatter(
        contract_last(dpre_all, weight_in), ("gx", "gz"), scatter_dimension=0, tiled=True
    ).astype(jnp.bfloat16)
    return (grad_inputs, grad_weight_in, grad_weight_out)


def solution(mesh):
    in_specs = (
        P(("gx", "gz"), "gy"),
        P("gy", ("gx", "gz")),
        P(("gx", "gz"), "gy"),
        P(("gx", "gz"), "gy"),
    )
    out_specs = (P(("gx", "gz"), "gy"), P("gy", ("gx", "gz")), P(("gx", "gz"), "gy"))
    return jax.shard_map(
        per_device, mesh=mesh, in_specs=in_specs, out_specs=out_specs, check_vma=False
    )
```

profile of v0, /device:TPU:1, one launch (start us, length us, event | category | flops | bytes accessed | tf_op | source)
XLA Modules:
  0.0 844.7 jit_solution(6826961527542970124)
XLA Ops:
  7.2 0.7 all-gather.7.cloned.1.call-update
  8.0 0.7 all-gather.5.cloned.1.call-update
  8.7 0.0 all-reduce.5.cloned.1.call-start
  8.7 191.4 %all-gather.7.cloned.1.call-done = bf16[64,7,1536]{2,1,0:T(8,128)(2,1)} async-done(((bf16[1,7,1536]{2,1,0:T(8,128)(2,1)}), bf16[64,7,1536]{2,1,0:T(8,128)(2,1)}) %all-gather.7.cloned.1.call-update) | async-done | bytes 1376272 | tf_op jit(solution)/shard_map/all_gather | solution.py:33
  200.2 2.4 reshape.9
  202.6 1.7 fusion.25
  204.3 0.0 reduce-scatter.6.cloned.1.call-start
  204.4 188.5 %all-gather.5.cloned.1.call-done = bf16[64,7,1536]{2,1,0:T(8,128)(2,1)} async-done(((bf16[1,7,1536]{2,1,0:T(8,128)(2,1)}), bf16[64,7,1536]{2,1,0:T(8,128)(2,1)}) %all-gather.5.cloned.1.call-update) | async-done | bytes 1376272 | tf_op jit(solution)/shard_map/all_gather | solution.py:34
  392.9 3.4 reshape.7
  396.3 3.4 fusion.24
  399.7 1.3 dynamic-slice.6
  401.6 121.9 %all-reduce.5.cloned.1.call-done = f32[448,384]{1,0:T(8,128)} async-done(((f32[448,384]{1,0:T(8,128)}), f32[448,384]{1,0:T(8,128)}) %all-reduce.5.cloned.1.call-update) | async-done | bytes 688144 | tf_op jit(solution)/shard_map/psum | solution.py:40
  523.6 94.5 %reduce-scatter.6.cloned.1.call-done = f32[56,384]{1,0:T(8,128)} async-done(((f32[448,384]{1,0:T(8,128)}), f32[56,384]{1,0:T(8,128)}) %reduce-scatter.6.cloned.1.call-update) | async-done | bytes 86032
  618.0 1.0 fusion.18
  619.0 39.6 %all_gather.11 = bf16[448,384]{1,0:T(8,128)(2,1)S(1)} all-gather(bf16[56,384]{1,0:T(8,128)(2,1)S(1)} %fusion.18), channel_id=1, replica_groups=mesh['gx'=8,'gy'=8,'gz'=8] {'gy'}, dimensions={0}, use_global_device_ids=true | all-gather | bytes 387072 | tf_op jit(solution)/shard_map/all_gather | solution.py:46
  658.6 2.4 fusion.26
  661.1 149.1 %fusion = f32[8,1536]{1,0:T(8,128)S(1)} fusion(f32[448,1536]{1,0:T(8,128)} %fusion.26), kind=kCustom, calls=%all-reduce-scatter | all-reduce-scatter fusion | flops 786433 | bytes 2803712
  810.2 1.9 collective-permute-start.1
  812.1 1.9 collective-permute-start.2
  814.0 1.9 collective-permute-start.7
  816.0 3.4 convolution_convert_fusion
  819.4 1.9 collective-permute-start.3
  821.3 1.9 collective-permute-start.4
  823.2 3.0 collective-permute-done.7
  826.2 1.9 collective-permute-start.5
  828.1 1.9 collective-permute-start.6
  830.1 2.0 collective-permute-start
  832.1 1.8 fusion.1
  834.0 2.4 copy.9
  836.4 0.1 collective-permute-done
  836.4 1.1 concatenate
  837.5 0.6 dynamic-slice_convert_fusion
  (14 shorter events, 0.1 us)
Async XLA Ops:
  7.2 195.4 %copy-start = (bf16[1536,384]{1,0:T(8,128)(2,1)S(1)}, bf16[1536,384]{1,0:T(8,128)(2,1)}, u32[]{:S(2)}) copy-start(bf16[1536,384]{1,0:T(8,128)(2,1)} %param.5) | copy-start | bytes 3538948
  7.2 193.0 %all-gather.7.cloned.1.call-start = ((), (), s32[]{:S(2)}) async-start(), calls=%async_computation.3 | async-start | bytes 1597440 | tf_op jit(solution)/shard_map/all_gather | solution.py:33
  7.9 385.0 %all-gather.5.cloned.1.call-start = ((), (), s32[]{:S(2)}) async-start(), calls=%async_computation.2 | async-start | bytes 1597440 | tf_op jit(solution)/shard_map/all_gather | solution.py:34
  8.7 514.9 %all-reduce.5.cloned.1.call-start = ((), (), s32[]{:S(2)}) async-start(), calls=%async_computation.1 | async-start | bytes 1376256 | tf_op jit(solution)/shard_map/psum | solution.py:40
  204.3 413.7 %reduce-scatter.6.cloned.1.call-start = ((), (), s32[]{:S(2)}) async-start(), calls=%async_computation.4 | async-start | bytes 774144
  810.2 18.0 %collective-permute-start.1 = (bf16[8,1536]{1,0:T(8,128)(2,1)S(1)}, bf16[8,1536]{1,0:T(8,128)(2,1)S(1)}, u32[]{:S(2)}, u32[]{:S(2)}) collective-permute-start(bf16[8,1536]{1,0:T(8,128)(2,1)S(1)} %convert.14), channel_id=1, source_target_pairs={{0,2},{1,3},{2,4},{3,5},{4,6},{5,7},{6,64},{7,65},{64,66},{65,67},... | collective-permute-start | bytes 73736
  812.1 18.0 %collective-permute-start.2 = (bf16[8,1536]{1,0:T(8,128)(2,1)S(1)}, bf16[8,1536]{1,0:T(8,128)(2,1)S(1)}, u32[]{:S(2)}, u32[]{:S(2)}) collective-permute-start(bf16[8,1536]{1,0:T(8,128)(2,1)S(1)} %convert.14), channel_id=1, source_target_pairs={{0,3},{1,4},{2,5},{3,6},{4,7},{5,64},{6,65},{7,66},{64,67},{65,68}... | collective-permute-start | bytes 73736
  814.0 12.2 %collective-permute-start.7 = (bf16[7,1536]{1,0:T(8,128)(2,1)S(1)}, bf16[7,1536]{1,0:T(8,128)(2,1)S(1)}, u32[]{:S(2)}, u32[]{:S(2)}) collective-permute-start(bf16[7,1536]{1,0:T(8,128)(2,1)S(1)} %slice), channel_id=1, source_target_pairs={{0,64},{1,65},{2,66},{3,67},{4,68},{5,69},{6,70},{7,71},{64,128},{... | collective-permute-start | bytes 64520
  819.4 17.0 %collective-permute-start.3 = (bf16[8,1536]{1,0:T(8,128)(2,1)S(1)}, bf16[8,1536]{1,0:T(8,128)(2,1)S(1)}, u32[]{:S(2)}, u32[]{:S(2)}) collective-permute-start(bf16[8,1536]{1,0:T(8,128)(2,1)S(1)} %convert.14), channel_id=1, source_target_pairs={{0,4},{1,5},{2,6},{3,7},{4,64},{5,65},{6,66},{7,67},{64,68},{65,69... | collective-permute-start | bytes 73736
  821.3 15.1 %collective-permute-start.4 = (bf16[8,1536]{1,0:T(8,128)(2,1)S(1)}, bf16[8,1536]{1,0:T(8,128)(2,1)S(1)}, u32[]{:S(2)}, u32[]{:S(2)}) collective-permute-start(bf16[8,1536]{1,0:T(8,128)(2,1)S(1)} %convert.14), channel_id=1, source_target_pairs={{0,5},{1,6},{2,7},{3,64},{4,65},{5,66},{6,67},{7,68},{64,69},{65,7... | collective-permute-start | bytes 73736
  826.2 10.1 %collective-permute-start.5 = (bf16[8,1536]{1,0:T(8,128)(2,1)S(1)}, bf16[8,1536]{1,0:T(8,128)(2,1)S(1)}, u32[]{:S(2)}, u32[]{:S(2)}) collective-permute-start(bf16[8,1536]{1,0:T(8,128)(2,1)S(1)} %convert.14), channel_id=1, source_target_pairs={{0,6},{1,7},{2,64},{3,65},{4,66},{5,67},{6,68},{7,69},{64,70},{65,... | collective-permute-start | bytes 73736
  828.1 8.2 collective-permute-start.6
  830.1 6.4 collective-permute-start
Sparse Core Ops, SparseCore 0:
  10.1 189.9 all-gather.6
  202.3 190.5 all-gather.4
  396.4 127.1 all-reduce.4
  528.5 89.4 reduce-scatter.5
where the time goes:
time: 858 us; the launch traced here: 845 us
  waiting for transfers between devices  601 us (70%)
  blocking collectives  189 us (22%)
  starting transfers between devices  15.6 us (2%)
  between operations  14.6 us (2%)
  matrix products  12.8 us (1%)
  local copies, waits for them, and re-layouts  11.1 us (1%)
    all_gather x1, waiting for transfers between devices, per_device(): lax.all_gather(inputs, ('gx', 'gz'), axis=0, tiled=True)  191 us
    all_gather x1, waiting for transfers between devices, per_device(): lax.all_gather(grad_output, ('gx', 'gz'), axis=0, tiled=True)  189 us
    unnamed x1, blocking collectives  149 us
    psum x1, waiting for transfers between devices, per_device(): pre_whole = lax.psum(pre_part, 'gy')  122 us
    unnamed x13, waiting for transfers between devices  99 us
    all_gather x1, blocking collectives, per_device(): dpre_all = lax.all_gather(dpre_own, 'gy', axis=0, tiled=True)  39.6 us
  transfers between devices with their start and end apart: 12, of which 6 were waited for; matrix products, arithmetic and copies ran while one was open for 2% of the time, Pallas kernels for 0%

commit v1 on v0

v1 whole, which is shorter than its diff:
```python
import jax
import jax.numpy as jnp
from jax import lax
from jax.sharding import PartitionSpec as P

coeff = 0.7978845608
bf16 = jnp.bfloat16
f32 = jnp.float32


def gelu_value(v):
    inner = jnp.tanh(coeff * (v + 0.044715 * v * v * v))
    return 0.5 * v * (1.0 + inner)


def gelu_slope(v):
    inner = jnp.tanh(coeff * (v + 0.044715 * v * v * v))
    return 0.5 * (1.0 + inner) + 0.5 * v * (1.0 - inner * inner) * coeff * (1.0 + 0.134145 * v * v)


def contract_last(left, right):
    return lax.dot_general(left, right, (((1,), (1,)), ((), ())), preferred_element_type=f32)


def contract_first(left, right):
    return lax.dot_general(left, right, (((0,), (0,)), ((), ())), preferred_element_type=f32)


def per_device(inputs, weight_in, weight_out, grad_output):
    nx, ny, nz = lax.axis_size("gx"), lax.axis_size("gy"), lax.axis_size("gz")
    rows, width = inputs.shape
    hidden = weight_in.shape[1]
    chips = nx // 2 * nz
    same_core = [[x * nz + z for x in range(core, nx, 2) for z in range(nz)] for core in range(2)]
    swap_cores = [(x, x ^ 1) for x in range(nx)]

    both = jnp.concatenate([inputs, grad_output], axis=0)
    spread = jnp.broadcast_to(both[None], (chips, 2 * rows, width))
    got = lax.all_to_all(spread, ("gx", "gz"), 0, 0, axis_index_groups=same_core)
    own_in = got[:, :rows].reshape(chips * rows, width)
    own_grad = got[:, rows:].reshape(chips * rows, width)
    own = jnp.concatenate([own_in, own_grad], axis=0)
    other = lax.ppermute(own, "gx", swap_cores)
    all_in = jnp.concatenate([own_in, other[: chips * rows]], axis=0)
    all_grad = jnp.concatenate([own_grad, other[chips * rows :]], axis=0)
    tokens = 2 * chips * rows
    share = tokens // ny

    pre_part = jnp.dot(all_in, weight_in, preferred_element_type=f32).astype(bf16)
    dact_part = contract_last(all_grad, weight_out).astype(bf16)
    parts = jnp.concatenate([pre_part, dact_part], axis=1).reshape(ny, share, 2 * hidden)
    parts = lax.all_to_all(parts, "gy", 0, 0)
    sums = jnp.sum(parts.astype(f32), axis=0)
    pre, dact = sums[:, :hidden], sums[:, hidden:]
    act = gelu_value(pre).astype(bf16)
    dpre = (dact * gelu_slope(pre)).astype(bf16)
    mine = jnp.concatenate([act, dpre], axis=1)
    spread = jnp.broadcast_to(mine[None], (ny, share, 2 * hidden))
    whole = lax.all_to_all(spread, "gy", 0, 0).reshape(tokens, 2 * hidden)
    act_all, dpre_all = whole[:, :hidden], whole[:, hidden:]

    half = chips * rows
    to_other = contract_last(dpre_all[half:], weight_in)
    from_other = lax.ppermute(to_other, "gx", swap_cores)
    chip_sum = (contract_last(dpre_all[:half], weight_in) + from_other).astype(bf16)
    pieces = lax.all_to_all(
        chip_sum.reshape(chips, rows, width), ("gx", "gz"), 0, 0, axis_index_groups=same_core
    )
    grad_inputs = jnp.sum(pieces.astype(f32), axis=0).astype(bf16)
    grad_weight_out = contract_first(act_all, all_grad).astype(bf16)
    grad_weight_in = contract_first(all_in, dpre_all).astype(bf16)
    return (grad_inputs, grad_weight_in, grad_weight_out)


def solution(mesh):
    in_specs = (
        P(("gx", "gz"), "gy"),
        P("gy", ("gx", "gz")),
        P(("gx", "gz"), "gy"),
        P(("gx", "gz"), "gy"),
    )
    out_specs = (P(("gx", "gz"), "gy"), P("gy", ("gx", "gz")), P(("gx", "gz"), "gy"))
    return jax.shard_map(
        per_device, mesh=mesh, in_specs=in_specs, out_specs=out_specs, check_vma=False
    )
```

time: 858 us -> 153 us (0.18); the launches traced: 845 us -> 152 us
  waiting for transfers between devices: 601 us -> 20.9 us
  blocking collectives: 189 us -> 90.1 us
  between operations: 14.6 us -> 0.83 us
  starting transfers between devices: 15.6 us -> 26.6 us
    all_gather x2 -> x0, waiting for transfers between devices: 380 us -> none  [the longest x1 191 us: per_device(): lax.all_gather(inputs, ('gx', 'gz'), axis=0, tiled=True)]
    unnamed x1 -> x0, blocking collectives: 149 us -> none
    psum x1 -> x0, waiting for transfers between devices: 122 us -> none  [per_device(): pre_whole = lax.psum(pre_part, 'gy')]
    unnamed x13 -> x0, waiting for transfers between devices: 99 us -> none
    all_to_all x0 -> x3, blocking collectives: none -> 90.1 us  [the longest x1 52.3 us: per_device(): lax.all_to_all(spread, ('gx', 'gz'), 0, 0, axis_index_groups=same_core)]
    all_gather x1 -> x0, blocking collectives: 39.6 us -> none  [per_device(): dpre_all = lax.all_gather(dpre_own, 'gy', axis=0, tiled=True)]
    unnamed x9 -> x0, starting transfers between devices: 15.5 us -> none
    all_to_all x0 -> x1, waiting for transfers between devices: none -> 15.4 us  [per_device(): lax.all_to_all(chip_sum.reshape(chips, rows, width), ('gx', 'gz'), 0, 0,...]
  transfers between devices with their start and end apart: 12 -> 3, of which waited for: 6 -> 3; matrix products, arithmetic and copies ran while one was open for 2% -> 3% of each run, Pallas kernels for 0% -> 0%
where the time goes in v1:
time: 153 us; the launch traced here: 152 us
  blocking collectives  90.1 us (59%)
  starting transfers between devices  26.6 us (17%)
  waiting for transfers between devices  20.9 us (14%)
  matrix products  8.09 us (5%)
  local copies, waits for them, and re-layouts  3.03 us (2%)
  other arithmetic  1.97 us (1%)
    all_to_all x1, blocking collectives, per_device(): lax.all_to_all(spread, ('gx', 'gz'), 0, 0, axis_index_groups=same_core)  52.3 us
    all_to_all x1, blocking collectives, per_device(): parts = lax.all_to_all(parts, 'gy', 0, 0)  23 us
    all_to_all x1, waiting for transfers between devices, per_device(): lax.all_to_all(chip_sum.reshape(chips, rows, width), ('gx', 'gz'), 0, 0,...  15.4 us
    all_to_all x1, blocking collectives, per_device(): whole = lax.all_to_all(spread, 'gy', 0, 0).reshape(tokens, 2 * hidden)  14.8 us
    all_to_all x1, starting transfers between devices, per_device(): lax.all_to_all(chip_sum.reshape(chips, rows, width), ('gx', 'gz'), 0, 0,...  14.4 us
    ppermute x1, starting transfers between devices, per_device(): from_other = lax.ppermute(to_other, 'gx', swap_cores)  7.58 us
    dot_general x2, matrix products, contract_first(): lax.dot_general(left, right, (((0,), (0,)), ((), ())), preferred_element_...  5.15 us
    ppermute x1, starting transfers between devices, per_device(): other = lax.ppermute(own, 'gx', swap_cores)  4.62 us
  transfers between devices with their start and end apart: 3, of which 3 were waited for; matrix products, arithmetic and copies ran while one was open for 3% of the time, Pallas kernels for 0%

profile of v1, /device:TPU:1, one launch (start us, length us, event | category | flops | bytes accessed | tf_op | source)
XLA Modules:
  0.0 151.5 jit_solution(773841770448898830)
XLA Ops:
  0.6 0.0 copy-start
  0.6 0.9 pad_maximum_fusion.9
  1.5 0.2 broadcast_in_dim.4
  1.7 52.3 %all_to_all.20 = bf16[32,14,1536]{2,1,0:T(8,128)(2,1)S(1)} all-to-all(bf16[32,14,1536]{2,1,0:T(8,128)(2,1)S(1)} %broadcast_in_dim.4), channel_id=1, replica_groups={{0,1,2,3,4,5,6,7,128,129,130,131,132,133,134,135,256,257,258,259,260,26..., dimensions={0} | all-to-all | bytes 2752512 | tf_op jit(solution)/shard_map/all_to_all | solution.py:39
  54.0 0.3 fusion.17
  54.2 0.2 reshape.24
  54.5 0.2 reshape.23
  54.7 0.1 pad_maximum_fusion
  54.8 4.6 %collective-permute-start = (bf16[448,1536]{1,0:T(8,128)(2,1)S(1)}, bf16[448,1536]{1,0:T(8,128)(2,1)S(1)}, u32[]{:S(2)}, u32[]{:S(2)}) collective-permute-start(bf16[448,1536]{1,0:T(8,128)(2,1)S(1)} %pad_maximum_fusion), channel_id=1, source_target_pairs={{0,64},{64,0},{128,192},{192,128},{256,320},{320,256},{384,448},{4... | collective-permute-start | bytes 4128776 | tf_op jit(solution)/shard_map/ppermute | solution.py:43
  59.4 2.7 %collective-permute-done = bf16[448,1536]{1,0:T(8,128)(2,1)S(1)} collective-permute-done((bf16[448,1536]{1,0:T(8,128)(2,1)S(1)}, bf16[448,1536]{1,0:T(8,128)(2,1)S(1)}, u32[]{:S(2)}, u32[]{:S(2)}) %collective-permute-start) | collective-permute-done | bytes 1376288 | tf_op jit(solution)/shard_map/ppermute | solution.py:43
  62.2 0.1 fusion.18
  62.3 0.0 copy-start.3
  62.3 0.0 copy-start.6
  62.3 0.9 convolution_convert_fusion.3
  63.2 0.9 copy-done.6
  64.1 0.9 convolution_convert_fusion.2
  65.0 0.1 pad_maximum_fusion.7
  65.0 23.0 %all_to_all.21 = bf16[8,56,768]{2,1,0:T(8,128)(2,1)S(1)} all-to-all(bf16[8,56,768]{2,1,0:T(8,128)(2,1)S(1)} %bitcast.6), channel_id=1, replica_groups=mesh['gx'=8,'gy'=8,'gz'=8] {'gy'}, dimensions={0} | all-to-all | bytes 1376256 | tf_op jit(solution)/shard_map/all_to_all | solution.py:52
  88.0 0.1 convert_reduce_fusion
  88.1 0.1 multiply_convert_fusion
  88.3 14.8 %all_to_all.22 = bf16[8,56,768]{2,1,0:T(8,128)(2,1)S(1)} all-to-all(bf16[8,56,768]{2,1,0:T(8,128)(2,1)S(1)} %broadcast_in_dim.5), channel_id=1, replica_groups=mesh['gx'=8,'gy'=8,'gz'=8] {'gy'}, dimensions={0} | all-to-all | bytes 1376256 | tf_op jit(solution)/shard_map/all_to_all | solution.py:59
  103.1 0.6 fusion.3
  103.7 7.6 %collective-permute-start.1 = (f32[224,1536]{1,0:T(8,128)S(1)}, f32[224,1536]{1,0:T(8,128)S(1)}, u32[]{:S(2)}, u32[]{:S(2)}) collective-permute-start(f32[224,1536]{1,0:T(8,128)S(1)} %fusion.3), channel_id=1, source_target_pairs={{0,64},{64,0},{128,192},{192,128},{256,320},{320,256},{384,448},{4... | collective-permute-start | bytes 4128776 | tf_op jit(solution)/shard_map/ppermute | solution.py:64
  111.3 2.7 %collective-permute-done.1 = f32[224,1536]{1,0:T(8,128)S(1)} collective-permute-done((f32[224,1536]{1,0:T(8,128)S(1)}, f32[224,1536]{1,0:T(8,128)S(1)}, u32[]{:S(2)}, u32[]{:S(2)}) %collective-permute-start.1) | collective-permute-done | bytes 1376288 | tf_op jit(solution)/shard_map/ppermute | solution.py:64
  114.0 0.6 fusion
  114.6 1.1 reshape.27
  115.7 14.4 %all-to-all-start.3 = ((bf16[32,7,1536]{2,1,0:T(8,128)(2,1)}), bf16[32,7,1536]{2,1,0:T(8,128)(2,1)S(1)}, u32[]{:S(2)}, u32[]{:S(2)}) async-start(bf16[32,7,1536]{2,1,0:T(8,128)(2,1)} %reshape.27), calls=%async_computation.3 | async-start | bytes 1572864 | tf_op jit(solution)/shard_map/all_to_all | solution.py:66
  130.1 0.0 copy-start.4
  130.2 3.1 %convolution_convert_fusion = bf16[384,1536]{1,0:T(8,128)(2,1)} fusion(bf16[224,1536]{1,0:T(8,128)(2,1)} %copy-done.5, bf16[224,1536]{1,0:T(8,128)(2,1)S(1)} %reshape.24, bf16[448,768]{1,0:T(8,128)(2,1)} %bitcast.9), kind=kOutput, calls=%fused_computation | convolution fusion | flops 531824640 | bytes 2899968 | tf_op jit(solution)/shard_map/dot_general | solution.py:26
  133.3 2.0 %convolution_convert_fusion.1 = bf16[1536,384]{1,0:T(8,128)(2,1)} fusion(bf16[224,1536]{1,0:T(8,128)(2,1)S(1)} %reshape.23, bf16[224,1536]{1,0:T(8,128)(2,1)S(1)} %copy-done.4, bf16[448,768]{1,0:T(8,128)(2,1)S(1)} %bitcast.10), kind=kOutput, calls=%fused_computation.1 | convolution fusion | flops 531824640 | bytes 2899968 | tf_op jit(solution)/shard_map/dot_general | solution.py:26
  135.3 15.4 %all-to-all-done.3 = bf16[32,7,1536]{2,1,0:T(8,128)(2,1)S(1)} async-done(((bf16[32,7,1536]{2,1,0:T(8,128)(2,1)}), bf16[32,7,1536]{2,1,0:T(8,128)(2,1)S(1)}, u32[]{:S(2)}, u32[]{:S(2)}) %all-to-all-start.3) | async-done | bytes 688160 | tf_op jit(solution)/shard_map/all_to_all | solution.py:66
  150.8 0.8 reduce_sum.22
  (11 shorter events, 0.1 us)
Async XLA Ops:
  0.6 61.7 %copy-start = (bf16[1536,384]{1,0:T(8,128)(2,1)S(1)}, bf16[1536,384]{1,0:T(8,128)(2,1)}, u32[]{:S(2)}) copy-start(bf16[1536,384]{1,0:T(8,128)(2,1)} %param.5) | copy-start | bytes 3538948
  54.8 7.4 %collective-permute-start = (bf16[448,1536]{1,0:T(8,128)(2,1)S(1)}, bf16[448,1536]{1,0:T(8,128)(2,1)S(1)}, u32[]{:S(2)}, u32[]{:S(2)}) collective-permute-start(bf16[448,1536]{1,0:T(8,128)(2,1)S(1)} %pad_maximum_fusion), channel_id=1, source_target_pairs={{0,64},{64,0},{128,192},{192,128},{256,320},{320,256},{384,448},{4... | collective-permute-start | bytes 4128776 | tf_op jit(solution)/shard_map/ppermute | solution.py:43
  62.3 0.9 copy-start.3
  62.3 2.7 %copy-start.5 = (bf16[224,1536]{1,0:T(8,128)(2,1)}, bf16[224,1536]{1,0:T(8,128)(2,1)S(1)}, u32[]{:S(2)}) copy-start(bf16[224,1536]{1,0:T(8,128)(2,1)S(1)} %get-tuple-element.6) | copy-start | bytes 2064388
  62.3 1.8 %copy-start.6 = (bf16[384,1536]{1,0:T(8,128)(2,1)S(1)}, bf16[384,1536]{1,0:T(8,128)(2,1)}, u32[]{:S(2)}) copy-start(bf16[384,1536]{1,0:T(8,128)(2,1)} %param.6) | copy-start | bytes 3538948
  103.1 10.9 %copy-start.1 = (bf16[8,56,768]{2,1,0:T(8,128)(2,1)}, bf16[8,56,768]{2,1,0:T(8,128)(2,1)S(1)}, u32[]{:S(2)}) copy-start(bf16[8,56,768]{2,1,0:T(8,128)(2,1)S(1)} %all_to_all.22) | copy-start | bytes 2064388
  103.7 10.3 %collective-permute-start.1 = (f32[224,1536]{1,0:T(8,128)S(1)}, f32[224,1536]{1,0:T(8,128)S(1)}, u32[]{:S(2)}, u32[]{:S(2)}) collective-permute-start(f32[224,1536]{1,0:T(8,128)S(1)} %fusion.3), channel_id=1, source_target_pairs={{0,64},{64,0},{128,192},{192,128},{256,320},{320,256},{384,448},{4... | collective-permute-start | bytes 4128776 | tf_op jit(solution)/shard_map/ppermute | solution.py:64
  115.7 35.0 %all-to-all-start.3 = ((bf16[32,7,1536]{2,1,0:T(8,128)(2,1)}), bf16[32,7,1536]{2,1,0:T(8,128)(2,1)S(1)}, u32[]{:S(2)}, u32[]{:S(2)}) async-start(bf16[32,7,1536]{2,1,0:T(8,128)(2,1)} %reshape.27), calls=%async_computation.3 | async-start | bytes 1572864 | tf_op jit(solution)/shard_map/all_to_all | solution.py:66
  130.1 3.1 %copy-start.2 = (bf16[8,56,768]{2,1,0:T(8,128)(2,1)S(1)}, bf16[8,56,768]{2,1,0:T(8,128)(2,1)}, u32[]{:S(2)}) copy-start(bf16[8,56,768]{2,1,0:T(8,128)(2,1)} %copy-done.1) | copy-start | bytes 2064388
  130.1 3.1 %copy-start.4 = (bf16[224,1536]{1,0:T(8,128)(2,1)S(1)}, bf16[224,1536]{1,0:T(8,128)(2,1)}, u32[]{:S(2)}) copy-start(bf16[224,1536]{1,0:T(8,128)(2,1)} %copy-done.3) | copy-start | bytes 2064388

commit v2 on v1

v2 whole, which is shorter than its diff:
```python
import jax
import jax.numpy as jnp
from jax import lax
from jax.sharding import PartitionSpec as P

coeff = 0.7978845608
bf16 = jnp.bfloat16
f32 = jnp.float32


def gelu_value(v):
    inner = jnp.tanh(coeff * (v + 0.044715 * v * v * v))
    return 0.5 * v * (1.0 + inner)


def gelu_slope(v):
    inner = jnp.tanh(coeff * (v + 0.044715 * v * v * v))
    return 0.5 * (1.0 + inner) + 0.5 * v * (1.0 - inner * inner) * coeff * (1.0 + 0.134145 * v * v)


def contract_last(left, right):
    return lax.dot_general(left, right, (((1,), (1,)), ((), ())), preferred_element_type=f32)


def contract_first(left, right):
    return lax.dot_general(left, right, (((0,), (0,)), ((), ())), preferred_element_type=f32)


def spread_groups(ny, nz):
    def at(y, core, z):
        return (2 * y + core) * nz + z

    first = [[at(y, 0, z) for z in range(nz)] for y in range(ny)]
    second = [[at(y, 0, z) for y in range(ny)] for z in range(nz)]
    pairs = nz // ny
    first += [
        [at(y, 1, lead + dz) for y in range(ny) for dz in range(pairs)] for lead in range(0, nz, pairs)
    ]
    second += [
        [at(y, 1, pairs * k + dz) for k in range(ny)] for y in range(ny) for dz in range(pairs)
    ]
    last = [
        [at(y, 0, z) for y in range(ny) for z in range(nz)],
        [at(y, 1, pairs * k + dz) for k in range(ny) for y in range(ny) for dz in range(pairs)],
    ]
    return first, second, last


def per_device(inputs, weight_in, weight_out, grad_output):
    nx, ny, nz = lax.axis_size("gx"), lax.axis_size("gy"), lax.axis_size("gz")
    rows, width = inputs.shape
    hidden = weight_in.shape[1]
    along = nx // 2
    chips = along * nz
    first, second, last = spread_groups(along, nz)
    swap_cores = [(x, x ^ 1) for x in range(nx)]

    def swap(v):
        return lax.ppermute(v, "gx", swap_cores)

    other_in, other_out = swap(weight_in), swap(weight_out)

    both = jnp.concatenate([inputs, grad_output], axis=0)
    got = lax.all_to_all(
        jnp.broadcast_to(both[None], (nz, 2 * rows, width)), ("gx", "gz"), 0, 0, axis_index_groups=first
    ).reshape(nz * 2 * rows, width)
    got = lax.all_to_all(
        jnp.broadcast_to(got[None], (along, nz * 2 * rows, width)),
        ("gx", "gz"), 0, 0, axis_index_groups=second,
    ).reshape(chips, 2 * rows, width)
    own_in = got[:, :rows].reshape(chips * rows, width)
    own_grad = got[:, rows:].reshape(chips * rows, width)
    tokens = chips * rows
    share = tokens // (ny // 2)

    swapped_in, swapped_grad = swap(own_in), swap(own_grad)

    def shares(v):
        return v.reshape(ny // 2, 1, share, hidden)

    pre_part = jnp.concatenate(
        [
            shares(jnp.dot(own_in, weight_in, preferred_element_type=f32).astype(bf16)),
            shares(jnp.dot(own_in, other_in, preferred_element_type=f32).astype(bf16)),
        ],
        axis=1,
    )
    dact_part = jnp.concatenate(
        [
            shares(contract_last(own_grad, weight_out).astype(bf16)),
            shares(contract_last(own_grad, other_out).astype(bf16)),
        ],
        axis=1,
    )
    parts = jnp.concatenate([pre_part, dact_part], axis=3).reshape(ny, share, 2 * hidden)
    parts = lax.all_to_all(parts, "gy", 0, 0)
    sums = jnp.sum(parts.astype(f32), axis=0)
    pre, dact = sums[:, :hidden], sums[:, hidden:]
    act = gelu_value(pre).astype(bf16)
    dpre = (dact * gelu_slope(pre)).astype(bf16)
    mine = jnp.concatenate([act, dpre], axis=1)
    whole = lax.all_to_all(jnp.broadcast_to(mine[None], (ny, share, 2 * hidden)), "gy", 0, 0)
    whole = whole.reshape(ny // 2, 2, share, 2 * hidden)
    own_whole = whole[:, 0].reshape(tokens, 2 * hidden)
    for_other = whole[:, 1].reshape(tokens, 2 * hidden)
    swapped_whole = swap(for_other)

    chip_sum = contract_last(own_whole[:, hidden:], weight_in) + contract_last(for_other[:, hidden:], other_in)
    pieces = lax.all_to_all(
        chip_sum.astype(bf16).reshape(chips, rows, width), ("gx", "gz"), 0, 0, axis_index_groups=last
    )
    grad_inputs = jnp.sum(pieces.astype(f32), axis=0).astype(bf16)
    grad_weight_out = (
        contract_first(own_whole[:, :hidden], own_grad)
        + contract_first(swapped_whole[:, :hidden], swapped_grad)
    ).astype(bf16)
    grad_weight_in = (
        contract_first(own_in, own_whole[:, hidden:])
        + contract_first(swapped_in, swapped_whole[:, hidden:])
    ).astype(bf16)
    return (grad_inputs, grad_weight_in, grad_weight_out)


def solution(mesh):
    in_specs = (
        P(("gx", "gz"), "gy"),
        P("gy", ("gx", "gz")),
        P(("gx", "gz"), "gy"),
        P(("gx", "gz"), "gy"),
    )
    out_specs = (P(("gx", "gz"), "gy"), P("gy", ("gx", "gz")), P(("gx", "gz"), "gy"))
    return jax.shard_map(
        per_device, mesh=mesh, in_specs=in_specs, out_specs=out_specs, check_vma=False
    )
```

time: 153 us -> 141 us (0.922)
  blocking collectives: 90.1 us -> 37.7 us
  starting transfers between devices: 26.6 us -> 49 us
  waiting for transfers between devices: 20.9 us -> 30.3 us
  matrix products: 8.09 us -> 15.2 us
    all_to_all x2 -> x1, blocking collectives: 67.1 us -> 15.4 us  [per_device(): lax.all_to_all(jnp.broadcast_to(both[None], (nz, 2 * rows, width)), ('gx'...]
    all_to_all x1 -> x3, starting transfers between devices: 14.4 us -> 28.9 us  [the longest x1 16.1 us: per_device(): lax.all_to_all(chip_sum.astype(bf16).reshape(chips, rows, width), ('gx',...]
    all_to_all x1 -> x3, waiting for transfers between devices: 15.4 us -> 29.8 us  [the longest x1 13.2 us: per_device(): lax.all_to_all(jnp.broadcast_to(got[None], (along, nz * 2 * rows, width))...]
    ppermute x2 -> x5, starting transfers between devices: 12.2 us -> 20.1 us  [swap(): return lax.ppermute(v, 'gx', swap_cores)]
    dot_general x3 -> x4, matrix products: 2.06 us -> 7.41 us  [contract_last(): lax.dot_general(left, right, (((1,), (1,)), ((), ())), preferred_element_...]
    ppermute x2 -> x5, waiting for transfers between devices: 5.47 us -> 0.51 us  [swap(): return lax.ppermute(v, 'gx', swap_cores)]
    dot_general x1 -> x2, matrix products: 0.87 us -> 3.57 us  [the longest x1 1.79 us: per_device(): jnp.dot(own_in, weight_in, preferred_element_type=f32).astype(bf16)]
    broadcast_in_dim x2 -> x4, local copies, waits for them, and re-layouts: 0.21 us -> 2.23 us  [the longest x2 1.31 us: per_device(): jnp.broadcast_to(got[None], (along, nz * 2 * rows, width))]
  transfers between devices with their start and end apart: 3 -> 8, of which waited for: 3 -> 4; matrix products, arithmetic and copies ran while one was open for 3% -> 11% of each run, Pallas kernels for 0% -> 0%
where the time goes in v2:
time: 141 us; the launch traced here: 139 us
  starting transfers between devices  49 us (35%)
  blocking collectives  37.7 us (27%)
  waiting for transfers between devices  30.3 us (21%)
  matrix products  15.2 us (11%)
  local copies, waits for them, and re-layouts  4.53 us (3%)
  other arithmetic  1.79 us (1%)
    all_to_all x1, blocking collectives, per_device(): parts = lax.all_to_all(parts, 'gy', 0, 0)  22.3 us
    ppermute x5, starting transfers between devices, swap(): return lax.ppermute(v, 'gx', swap_cores)  20.1 us
    all_to_all x1, starting transfers between devices, per_device(): lax.all_to_all(chip_sum.astype(bf16).reshape(chips, rows, width), ('gx',...  16.1 us
    all_to_all x1, blocking collectives, per_device(): lax.all_to_all(jnp.broadcast_to(both[None], (nz, 2 * rows, width)), ('gx'...  15.4 us
    all_to_all x1, waiting for transfers between devices, per_device(): lax.all_to_all(jnp.broadcast_to(got[None], (along, nz * 2 * rows, width))...  13.2 us
    all_to_all x1, waiting for transfers between devices, per_device(): lax.all_to_all(chip_sum.astype(bf16).reshape(chips, rows, width), ('gx',...  11.9 us
    all_to_all x1, starting transfers between devices, per_device(): lax.all_to_all(jnp.broadcast_to(got[None], (along, nz * 2 * rows, width))...  9.31 us
    dot_general x4, matrix products, contract_last(): lax.dot_general(left, right, (((1,), (1,)), ((), ())), preferred_element_...  7.41 us
  transfers between devices with their start and end apart: 8, of which 4 were waited for; matrix products, arithmetic and copies ran while one was open for 11% of the time, Pallas kernels for 0%

profile of v2, /device:TPU:1, one launch (start us, length us, event | category | flops | bytes accessed | tf_op | source)
XLA Modules:
  0.0 139.4 jit_solution(3364848651622192790)
XLA Ops:
  0.6 0.8 pad_maximum_fusion.1
  1.4 15.4 %all_to_all.25 = bf16[8,14,1536]{2,1,0:T(8,128)(2,1)S(1)} all-to-all(bf16[8,14,1536]{2,1,0:T(8,128)(2,1)S(1)} %broadcast_in_dim.8), channel_id=1, replica_groups={{0,1,2,3,4,5,6,7},{128,129,130,131,132,133,134,135},{256,257,258,259,26..., dimensions={0} | all-to-all | bytes 688128 | tf_op jit(solution)/shard_map/all_to_all | solution.py:64
  17.0 1.2 broadcast_in_dim.10
  18.2 9.3 %all-to-all-start.1 = ((bf16[4,112,1536]{2,1,0:T(8,128)(2,1)}), bf16[4,112,1536]{2,1,0:T(8,128)(2,1)S(1)}, u32[]{:S(2)}, u32[]{:S(2)}) async-start(bf16[4,112,1536]{2,1,0:T(8,128)(2,1)} %broadcast_in_dim.10), calls=%async_computation.1 | async-start | bytes 2752512 | tf_op jit(solution)/shard_map/all_to_all | solution.py:67
  27.5 5.7 %collective-permute-start.1 = (bf16[384,1536]{1,0:T(8,128)(2,1)}, bf16[384,1536]{1,0:T(8,128)(2,1)}, u32[]{:S(2)}, u32[]{:S(2)}) collective-permute-start(bf16[384,1536]{1,0:T(8,128)(2,1)} %param.6), channel_id=1, source_target_pairs={{0,64},{64,0},{128,192},{192,128},{256,320},{320,256},{384,448},{4... | collective-permute-start | bytes 3538952 | tf_op jit(solution)/shard_map/ppermute | solution.py:59
  33.2 1.9 %collective-permute-start = (bf16[1536,384]{1,0:T(8,128)(2,1)}, bf16[1536,384]{1,0:T(8,128)(2,1)}, u32[]{:S(2)}, u32[]{:S(2)}) collective-permute-start(bf16[1536,384]{1,0:T(8,128)(2,1)} %param.5), channel_id=1, source_target_pairs={{0,64},{64,0},{128,192},{192,128},{256,320},{320,256},{384,448},{4... | collective-permute-start | bytes 3538952 | tf_op jit(solution)/shard_map/ppermute | solution.py:59
  35.2 13.2 %all-to-all-done.1 = bf16[4,112,1536]{2,1,0:T(8,128)(2,1)S(1)} async-done(((bf16[4,112,1536]{2,1,0:T(8,128)(2,1)}), bf16[4,112,1536]{2,1,0:T(8,128)(2,1)S(1)}, u32[]{:S(2)}, u32[]{:S(2)}) %all-to-all-start.1) | async-done | bytes 1376288 | tf_op jit(solution)/shard_map/all_to_all | solution.py:67
  48.3 0.4 reshape.39
  48.8 0.3 fusion.19
  49.0 0.2 reshape.43
  49.5 1.8 %convolution_convert_fusion.1 = bf16[224,384]{1,0:T(8,128)(2,1)S(1)} fusion(bf16[224,1536]{1,0:T(8,128)(2,1)S(1)} %reshape.43, bf16[384,1536]{1,0:T(8,128)(2,1)} %param.6), kind=kOutput, calls=%fused_computation.8 | convolution fusion | flops 264327168 | bytes 2039808 | tf_op jit(solution)/shard_map/dot_general | solution.py:22
  51.4 1.8 %convolution_convert_fusion.3 = bf16[224,384]{1,0:T(8,128)(2,1)S(1)} fusion(bf16[224,1536]{1,0:T(8,128)(2,1)S(1)} %reshape.40, bf16[1536,384]{1,0:T(8,128)(2,1)} %param.5), kind=kOutput, calls=%fused_computation.10 | convolution fusion | flops 264327168 | bytes 2039808 | tf_op jit(solution)/shard_map/dot_general | solution.py:83
  53.2 1.9 %convolution_convert_fusion = bf16[224,384]{1,0:T(8,128)(2,1)S(1)} fusion(bf16[224,1536]{1,0:T(8,128)(2,1)S(1)} %reshape.43, bf16[384,1536]{1,0:T(8,128)(2,1)} %collective-permute-done.1), kind=kOutput, calls=%fused_computation.7 | convolution fusion | flops 264327168 | bytes 2039808 | tf_op jit(solution)/shard_map/dot_general | solution.py:22
  55.0 1.8 %convolution_convert_fusion.2 = bf16[224,384]{1,0:T(8,128)(2,1)S(1)} fusion(bf16[224,1536]{1,0:T(8,128)(2,1)S(1)} %reshape.40, bf16[1536,384]{1,0:T(8,128)(2,1)} %collective-permute-done), kind=kOutput, calls=%fused_computation.9 | convolution fusion | flops 264327168 | bytes 2039808 | tf_op jit(solution)/shard_map/dot_general | solution.py:84
  56.9 22.3 %all_to_all.26 = bf16[8,56,768]{2,1,0:T(8,128)(2,1)S(1)} all-to-all(bf16[8,56,768]{2,1,0:T(8,128)(2,1)S(1)} %bitcast.31), channel_id=1, replica_groups=mesh['gx'=8,'gy'=8,'gz'=8] {'gy'}, dimensions={0} | all-to-all | bytes 1376256 | tf_op jit(solution)/shard_map/all_to_all | solution.py:96
  79.4 0.9 broadcast_in_dim.22
  80.3 3.5 %all-to-all-start.3 = ((bf16[8,56,768]{2,1,0:T(8,128)(2,1)}), bf16[8,56,768]{2,1,0:T(8,128)(2,1)S(1)}, u32[]{:S(2)}, u32[]{:S(2)}) async-start(bf16[8,56,768]{2,1,0:T(8,128)(2,1)} %broadcast_in_dim.22), calls=%async_computation.3 | async-start | bytes 1376256 | tf_op jit(solution)/shard_map/all_to_all | solution.py:102
  83.8 7.8 %collective-permute-start.2 = (bf16[224,1536]{1,0:T(8,128)(2,1)S(1)}, bf16[224,1536]{1,0:T(8,128)(2,1)S(1)}, u32[]{:S(2)}, u32[]{:S(2)}) collective-permute-start(bf16[224,1536]{1,0:T(8,128)(2,1)S(1)} %reshape.40), channel_id=1, source_target_pairs={{0,64},{64,0},{128,192},{192,128},{256,320},{320,256},{384,448},{4... | collective-permute-start | bytes 2064392 | tf_op jit(solution)/shard_map/ppermute | solution.py:59
  91.6 4.7 %all-to-all-done.3 = bf16[8,56,768]{2,1,0:T(8,128)(2,1)S(1)} async-done(((bf16[8,56,768]{2,1,0:T(8,128)(2,1)}), bf16[8,56,768]{2,1,0:T(8,128)(2,1)S(1)}, u32[]{:S(2)}, u32[]{:S(2)}) %all-to-all-start.3) | async-done | bytes 688160 | tf_op jit(solution)/shard_map/all_to_all | solution.py:102
  96.4 1.9 %fusion.10 = f32[224,1536]{1,0:T(8,128)S(1)} fusion(bf16[1536,384]{1,0:T(8,128)(2,1)} %param.5, bf16[224,768]{1,0:T(8,128)(2,1)S(1)} %bitcast.32), kind=kOutput, calls=%fused_computation.19 | convolution fusion | flops 264241152 | bytes 2727936 | tf_op jit(solution)/shard_map/dot_general | solution.py:22
  98.3 1.9 %fusion.2 = bf16[224,1536]{1,0:T(8,128)(2,1)S(1)} fusion(f32[224,1536]{1,0:T(8,128)S(1)} %fusion.10, bf16[1536,384]{1,0:T(8,128)(2,1)} %collective-permute-done, bf16[224,768]{1,0:T(8,128)(2,1)S(1)} %bitcast.35), kind=kOutput, calls=%fused_computation.5 | convolution fusion | flops 264929280 | bytes 3416064 | tf_op jit(solution)/shard_map/dot_general | solution.py:22
  100.2 1.1 reshape.48
  101.3 16.1 %all-to-all-start.4 = ((bf16[32,7,1536]{2,1,0:T(8,128)(2,1)}), bf16[32,7,1536]{2,1,0:T(8,128)(2,1)S(1)}, u32[]{:S(2)}, u32[]{:S(2)}) async-start(bf16[32,7,1536]{2,1,0:T(8,128)(2,1)} %reshape.48), calls=%async_computation.4 | async-start | bytes 1572864 | tf_op jit(solution)/shard_map/all_to_all | solution.py:109
  117.3 2.7 %collective-permute-start.4 = (bf16[224,1536]{1,0:T(8,128)(2,1)S(1)}, bf16[224,1536]{1,0:T(8,128)(2,1)S(1)}, u32[]{:S(2)}, u32[]{:S(2)}) collective-permute-start(bf16[224,1536]{1,0:T(8,128)(2,1)S(1)} %reshape.43), channel_id=1, source_target_pairs={{0,64},{64,0},{128,192},{192,128},{256,320},{320,256},{384,448},{4... | collective-permute-start | bytes 2064392 | tf_op jit(solution)/shard_map/ppermute | solution.py:59
  120.1 1.9 %collective-permute-start.3 = (bf16[224,768]{1,0:T(8,128)(2,1)S(1)}, bf16[224,768]{1,0:T(8,128)(2,1)S(1)}, u32[]{:S(2)}, u32[]{:S(2)}) collective-permute-start(bf16[224,768]{1,0:T(8,128)(2,1)S(1)} %bitcast.36), channel_id=1, source_target_pairs={{0,64},{64,0},{128,192},{192,128},{256,320},{320,256},{384,448},{4... | collective-permute-start | bytes 1032200 | tf_op jit(solution)/shard_map/ppermute | solution.py:59
  122.0 0.6 fusion.8
  122.6 0.5 fusion.4
  123.1 0.5 collective-permute-done.3
  123.6 1.6 %fusion = bf16[1536,384]{1,0:T(8,128)(2,1)} fusion(f32[1536,384]{1,0:T(8,128)S(1)} %fusion.8, bf16[224,1536]{1,0:T(8,128)(2,1)S(1)} %collective-permute-done.2, bf16[224,768]{1,0:T(8,128)(2,1)S(1)} %collective-permute-done.3), kind=kOutput, calls=%fused_computation.2 | convolution fusion | flops 265420800 | bytes 4399104 | tf_op jit(solution)/shard_map/dot_general | solution.py:26
  125.3 1.5 %fusion.1 = bf16[384,1536]{1,0:T(8,128)(2,1)} fusion(f32[384,1536]{1,0:T(8,128)S(1)} %fusion.4, bf16[224,1536]{1,0:T(8,128)(2,1)S(1)} %collective-permute-done.4, bf16[224,768]{1,0:T(8,128)(2,1)S(1)} %collective-permute-done.3), kind=kOutput, calls=%fused_computation.3 | convolution fusion | flops 265420800 | bytes 4399104 | tf_op jit(solution)/shard_map/dot_general | solution.py:26
  126.8 11.9 %all-to-all-done.4 = bf16[32,7,1536]{2,1,0:T(8,128)(2,1)S(1)} async-done(((bf16[32,7,1536]{2,1,0:T(8,128)(2,1)}), bf16[32,7,1536]{2,1,0:T(8,128)(2,1)S(1)}, u32[]{:S(2)}, u32[]{:S(2)}) %all-to-all-start.4) | async-done | bytes 688160 | tf_op jit(solution)/shard_map/all_to_all | solution.py:109
  138.7 0.8 reduce_sum.22
  (12 shorter events, 0.7 us)
Async XLA Ops:
  18.2 30.1 %all-to-all-start.1 = ((bf16[4,112,1536]{2,1,0:T(8,128)(2,1)}), bf16[4,112,1536]{2,1,0:T(8,128)(2,1)S(1)}, u32[]{:S(2)}, u32[]{:S(2)}) async-start(bf16[4,112,1536]{2,1,0:T(8,128)(2,1)} %broadcast_in_dim.10), calls=%async_computation.1 | async-start | bytes 2752512 | tf_op jit(solution)/shard_map/all_to_all | solution.py:67
  27.5 25.6 %collective-permute-start.1 = (bf16[384,1536]{1,0:T(8,128)(2,1)}, bf16[384,1536]{1,0:T(8,128)(2,1)}, u32[]{:S(2)}, u32[]{:S(2)}) collective-permute-start(bf16[384,1536]{1,0:T(8,128)(2,1)} %param.6), channel_id=1, source_target_pairs={{0,64},{64,0},{128,192},{192,128},{256,320},{320,256},{384,448},{4... | collective-permute-start | bytes 3538952 | tf_op jit(solution)/shard_map/ppermute | solution.py:59
  33.2 21.8 %collective-permute-start = (bf16[1536,384]{1,0:T(8,128)(2,1)}, bf16[1536,384]{1,0:T(8,128)(2,1)}, u32[]{:S(2)}, u32[]{:S(2)}) collective-permute-start(bf16[1536,384]{1,0:T(8,128)(2,1)} %param.5), channel_id=1, source_target_pairs={{0,64},{64,0},{128,192},{192,128},{256,320},{320,256},{384,448},{4... | collective-permute-start | bytes 3538952 | tf_op jit(solution)/shard_map/ppermute | solution.py:59
  80.3 16.1 %all-to-all-start.3 = ((bf16[8,56,768]{2,1,0:T(8,128)(2,1)}), bf16[8,56,768]{2,1,0:T(8,128)(2,1)S(1)}, u32[]{:S(2)}, u32[]{:S(2)}) async-start(bf16[8,56,768]{2,1,0:T(8,128)(2,1)} %broadcast_in_dim.22), calls=%async_computation.3 | async-start | bytes 1376256 | tf_op jit(solution)/shard_map/all_to_all | solution.py:102
  83.8 39.3 %collective-permute-start.2 = (bf16[224,1536]{1,0:T(8,128)(2,1)S(1)}, bf16[224,1536]{1,0:T(8,128)(2,1)S(1)}, u32[]{:S(2)}, u32[]{:S(2)}) collective-permute-start(bf16[224,1536]{1,0:T(8,128)(2,1)S(1)} %reshape.40), channel_id=1, source_target_pairs={{0,64},{64,0},{128,192},{192,128},{256,320},{320,256},{384,448},{4... | collective-permute-start | bytes 2064392 | tf_op jit(solution)/shard_map/ppermute | solution.py:59
  101.3 37.4 %all-to-all-start.4 = ((bf16[32,7,1536]{2,1,0:T(8,128)(2,1)}), bf16[32,7,1536]{2,1,0:T(8,128)(2,1)S(1)}, u32[]{:S(2)}, u32[]{:S(2)}) async-start(bf16[32,7,1536]{2,1,0:T(8,128)(2,1)} %reshape.48), calls=%async_computation.4 | async-start | bytes 1572864 | tf_op jit(solution)/shard_map/all_to_all | solution.py:109
  117.3 7.9 %collective-permute-start.4 = (bf16[224,1536]{1,0:T(8,128)(2,1)S(1)}, bf16[224,1536]{1,0:T(8,128)(2,1)S(1)}, u32[]{:S(2)}, u32[]{:S(2)}) collective-permute-start(bf16[224,1536]{1,0:T(8,128)(2,1)S(1)} %reshape.43), channel_id=1, source_target_pairs={{0,64},{64,0},{128,192},{192,128},{256,320},{320,256},{384,448},{4... | collective-permute-start | bytes 2064392 | tf_op jit(solution)/shard_map/ppermute | solution.py:59
  120.1 3.5 %collective-permute-start.3 = (bf16[224,768]{1,0:T(8,128)(2,1)S(1)}, bf16[224,768]{1,0:T(8,128)(2,1)S(1)}, u32[]{:S(2)}, u32[]{:S(2)}) collective-permute-start(bf16[224,768]{1,0:T(8,128)(2,1)S(1)} %bitcast.36), channel_id=1, source_target_pairs={{0,64},{64,0},{128,192},{192,128},{256,320},{320,256},{384,448},{4... | collective-permute-start | bytes 1032200 | tf_op jit(solution)/shard_map/ppermute | solution.py:59

commit v3 on v1

v3 whole, which is shorter than its diff:
```python
import jax
import jax.numpy as jnp
from jax import lax
from jax.sharding import PartitionSpec as P

coeff = 0.7978845608
bf16 = jnp.bfloat16
f16 = jnp.float16
f32 = jnp.float32


def gelu_value(v):
    inner = jnp.tanh(coeff * (v + 0.044715 * v * v * v))
    return 0.5 * v * (1.0 + inner)


def gelu_slope(v):
    inner = jnp.tanh(coeff * (v + 0.044715 * v * v * v))
    return 0.5 * (1.0 + inner) + 0.5 * v * (1.0 - inner * inner) * coeff * (1.0 + 0.134145 * v * v)


def contract_last(left, right):
    return lax.dot_general(left, right, (((1,), (1,)), ((), ())), preferred_element_type=f32)


def contract_first(left, right):
    return lax.dot_general(left, right, (((0,), (0,)), ((), ())), preferred_element_type=f32)


def pack(sums):
    columns = sums.shape[-1]
    kinds = sums.reshape(-1, 2, columns // 2)
    most = jnp.maximum(jnp.max(jnp.abs(kinds), axis=(0, 2)), 1e-30)
    power = jnp.repeat(jnp.round(jnp.log2(most)), columns // 2)
    tail = jnp.broadcast_to(power, (*sums.shape[:-2], 8, columns))
    return jnp.concatenate([(sums * jnp.exp2(13.0 - power)).astype(f16), tail.astype(f16)], axis=-2)


def unpack(packed):
    power = packed[..., -8:-7, :].astype(f32)
    return packed[..., :-8, :].astype(f32) * jnp.exp2(power - 13.0)


class Routes:
    def __init__(self, ny, nz):
        def at(y, core, z):
            return (2 * (y % ny) + core) * nz + z % nz

        self.blocks = ny
        self.first = [[at(y, 0, z) for z in range(nz)] for y in range(ny)] + [
            [at(y, 1, z + d * ny) for y in range(ny) for d in range(nz // ny)] for z in range(ny)
        ]

        def shift(dy, dz):
            return [(at(y + dy, 0, z), at(y, 0, z)) for y in range(ny) for z in range(nz)] + [
                (at(y, 1, z + dz), at(y, 1, z)) for y in range(ny) for z in range(nz)
            ]

        far = ny // 2
        self.moves = [(b, shift(b, b if b <= far else b - ny)) for b in [far, *range(1, far), *range(far + 1, ny)]]

    def send(self, source, axes):
        return {b: lax.ppermute(source, axes, pairs) for b, pairs in self.moves}

    def send_back(self, sources, axes):
        return [lax.ppermute(sources[b], axes, [(d, s) for s, d in pairs]) for b, pairs in self.moves]


def per_device(inputs, weight_in, weight_out, grad_output):
    nx, ny, nz = lax.axis_size("gx"), lax.axis_size("gy"), lax.axis_size("gz")
    rows, width = inputs.shape
    hidden = weight_in.shape[1]
    routes = Routes(nx // 2, nz)
    blocks = routes.blocks
    swap_cores = [(x, x ^ 1) for x in range(nx)]

    def swap(v):
        return lax.ppermute(v, "gx", swap_cores)

    halves = 2
    same_half = [[x * halves + h for x in range(ny // halves)] for h in range(halves)]
    other_half = [(g, g ^ 1) for g in range(ny)]

    both = jnp.concatenate([inputs, grad_output], axis=0)
    near = lax.all_to_all(
        jnp.broadcast_to(both[None], (nz, 2 * rows, width)), ("gx", "gz"), 0, 0, axis_index_groups=routes.first
    )
    share = nz * rows
    near = jnp.concatenate(
        [near[:, :rows].reshape(share, width), near[:, rows:].reshape(share, width)], axis=1
    )
    chip_in = jnp.concatenate([weight_in, swap(weight_in)], axis=1)
    chip_out = jnp.concatenate([weight_out, swap(weight_out)], axis=0)
    chip_in, chip_out = lax.optimization_barrier((chip_in, chip_out))
    found = routes.send(near, ("gx", "gz"))
    own = jnp.concatenate([near] + [found[b] for b in range(1, blocks)], axis=0)
    own_in, own_grad = own[:, :width], own[:, width:]
    swapped = swap(own)
    tokens = blocks * share

    pre_part = jnp.dot(own_in, chip_in, preferred_element_type=f32)
    dact_part = contract_last(own_grad, chip_out)
    parts = pack(jnp.concatenate([pre_part, dact_part], axis=1).reshape(blocks, share, 4 * hidden))
    parts = lax.all_to_all(parts, "gy", 0, 0, axis_index_groups=same_half)
    sums = jnp.sum(unpack(parts), axis=0)
    sums = sums + unpack(lax.ppermute(pack(sums), "gy", other_half))
    pre, dact = sums[:, : 2 * hidden], sums[:, 2 * hidden :]
    act = gelu_value(pre).astype(bf16)
    dpre = (dact * gelu_slope(pre)).astype(bf16)
    mine = jnp.concatenate([act, dpre], axis=1)
    whole = lax.all_to_all(
        jnp.broadcast_to(mine[None], (blocks, share, 4 * hidden)), "gy", 0, 0, axis_index_groups=same_half
    ).reshape(tokens, 4 * hidden)
    act_own, act_other = whole[:, :hidden], whole[:, hidden : 2 * hidden]
    dpre_own, dpre_other = whole[:, 2 * hidden : 3 * hidden], whole[:, 3 * hidden :]

    chip_sum = contract_last(whole[:, 2 * hidden :], chip_in).astype(bf16)
    for_other, chip_sum = lax.optimization_barrier(
        (jnp.concatenate([act_other, dpre_other], axis=1), chip_sum)
    )
    chip_sum = chip_sum.reshape(blocks, share, width)
    total = chip_sum[0].astype(f32)
    for v in routes.send_back(chip_sum, ("gx", "gz")):
        total = total + v.astype(f32)
    swapped_whole = swap(for_other)
    pieces = lax.all_to_all(
        total.astype(bf16).reshape(nz, rows, width), ("gx", "gz"), 0, 0, axis_index_groups=routes.first
    )
    grad_inputs = jnp.sum(pieces.astype(f32), axis=0).astype(bf16)
    grad_weight_out = (
        contract_first(act_own, own_grad) + contract_first(swapped_whole[:, :hidden], swapped[:, width:])
    ).astype(bf16)
    grad_weight_in = (
        contract_first(own_in, dpre_own) + contract_first(swapped[:, :width], swapped_whole[:, hidden:])
    ).astype(bf16)
    return (grad_inputs, grad_weight_in, grad_weight_out)


def solution(mesh):
    in_specs = (
        P(("gx", "gz"), "gy"),
        P("gy", ("gx", "gz")),
        P(("gx", "gz"), "gy"),
        P(("gx", "gz"), "gy"),
    )
    out_specs = (P(("gx", "gz"), "gy"), P("gy", ("gx", "gz")), P(("gx", "gz"), "gy"))
    return jax.shard_map(
        per_device, mesh=mesh, in_specs=in_specs, out_specs=out_specs, check_vma=False
    )
```

time: 153 us -> 133 us (0.87)
  blocking collectives: 90.1 us -> 12.9 us
  starting transfers between devices: 26.6 us -> 64.2 us
  waiting for transfers between devices: 20.9 us -> 34.3 us
  other arithmetic: 1.97 us -> 7.43 us
    all_to_all x3 -> x1, blocking collectives: 90.1 us -> 12.9 us  [per_device(): parts = lax.all_to_all(parts, 'gy', 0, 0, axis_index_groups=same_half)]
    ppermute x2 -> x11, starting transfers between devices: 12.2 us -> 40.6 us  [the longest x3 14.7 us: send_back(): lax.ppermute(sources[b], axes, [(d, s) for s, d in pairs])]
    ppermute x2 -> x11, waiting for transfers between devices: 5.47 us -> 19.4 us  [the longest x3 10.9 us: send(): return {b: lax.ppermute(source, axes, pairs) for b, pairs in self.moves}]
    all_to_all x1 -> x3, starting transfers between devices: 14.4 us -> 23.6 us  [the longest x1 13.9 us: per_device(): lax.all_to_all(jnp.broadcast_to(both[None], (nz, 2 * rows, width)), ('gx'...]
    concatenate x1 -> x6, other arithmetic: 0.09 us -> 2.49 us  [the longest x1 1.98 us: per_device(): chip_in = jnp.concatenate([weight_in, swap(weight_in)], axis=1)]
    broadcast_in_dim x2 -> x8, local copies, waits for them, and re-layouts: 0.21 us -> 1.98 us  [the longest x1 0.89 us: per_device(): jnp.broadcast_to(mine[None], (blocks, share, 4 * hidden))]
    convert_element_type x0 -> x3, other arithmetic: none -> 1.6 us  [the longest x2 1.5 us: pack(): (sums * jnp.exp2(13.0 - power)).astype(f16)]
    dot_general x2 -> x4, matrix products: 5.15 us -> 6.57 us  [contract_first(): lax.dot_general(left, right, (((0,), (0,)), ((), ())), preferred_element_...]
  transfers between devices with their start and end apart: 3 -> 14, of which waited for: 3 -> 8; matrix products, arithmetic and copies ran while one was open for 3% -> 8% of each run, Pallas kernels for 0% -> 0%
where the time goes in v3:
time: 133 us; the launch traced here: 132 us
  starting transfers between devices  64.2 us (48%)
  waiting for transfers between devices  34.3 us (26%)
  blocking collectives  12.9 us (10%)
  matrix products  9 us (7%)
  other arithmetic  7.43 us (6%)
  local copies, waits for them, and re-layouts  3.24 us (2%)
    ppermute x3, starting transfers between devices, send_back(): lax.ppermute(sources[b], axes, [(d, s) for s, d in pairs])  14.7 us
    all_to_all x1, starting transfers between devices, per_device(): lax.all_to_all(jnp.broadcast_to(both[None], (nz, 2 * rows, width)), ('gx'...  13.9 us
    all_to_all x1, blocking collectives, per_device(): parts = lax.all_to_all(parts, 'gy', 0, 0, axis_index_groups=same_half)  12.9 us
    ppermute x4, starting transfers between devices, swap(): return lax.ppermute(v, 'gx', swap_cores)  12.7 us
    ppermute x3, waiting for transfers between devices, send(): return {b: lax.ppermute(source, axes, pairs) for b, pairs in self.moves}  10.9 us
    ppermute x3, starting transfers between devices, send(): return {b: lax.ppermute(source, axes, pairs) for b, pairs in self.moves}  8.55 us
    all_to_all x1, waiting for transfers between devices, per_device(): lax.all_to_all(jnp.broadcast_to(both[None], (nz, 2 * rows, width)), ('gx'...  8.16 us
    ppermute x1, waiting for transfers between devices, per_device(): sums = sums + unpack(lax.ppermute(pack(sums), 'gy', other_half))  7.8 us
  transfers between devices with their start and end apart: 14, of which 8 were waited for; matrix products, arithmetic and copies ran while one was open for 8% of the time, Pallas kernels for 0%

profile of v3, /device:TPU:1, one launch (start us, length us, event | category | flops | bytes accessed | tf_op | source)
XLA Modules:
  0.0 132.1 jit_solution(1278278662843684264)
XLA Ops:
  2.2 13.9 %all-to-all-start = ((bf16[8,14,1536]{2,1,0:T(8,128)(2,1)}), bf16[8,14,1536]{2,1,0:T(8,128)(2,1)S(1)}, u32[]{:S(2)}, u32[]{:S(2)}) async-start(bf16[8,14,1536]{2,1,0:T(8,128)(2,1)} %broadcast_in_dim.30), calls=%async_computation | async-start | bytes 786432 | tf_op jit(solution)/shard_map/all_to_all | solution.py:85
  16.1 1.9 %collective-permute-start.3 = (bf16[1536,384]{1,0:T(8,128)(2,1)}, bf16[1536,384]{1,0:T(8,128)(2,1)}, u32[]{:S(2)}, u32[]{:S(2)}) collective-permute-start(bf16[1536,384]{1,0:T(8,128)(2,1)} %param.5), channel_id=1, source_target_pairs={{0,64},{64,0},{128,192},{192,128},{256,320},{320,256},{384,448},{4... | collective-permute-start | bytes 3538952 | tf_op jit(solution)/shard_map/ppermute | solution.py:78
  18.0 2.4 %collective-permute-start.4 = (bf16[384,1536]{1,0:T(8,128)(2,1)}, bf16[384,1536]{1,0:T(8,128)(2,1)S(1)}, u32[]{:S(2)}, u32[]{:S(2)}) collective-permute-start(bf16[384,1536]{1,0:T(8,128)(2,1)} %param.6), channel_id=1, source_target_pairs={{0,64},{64,0},{128,192},{192,128},{256,320},{320,256},{384,448},{4... | collective-permute-start | bytes 3538952 | tf_op jit(solution)/shard_map/ppermute | solution.py:78
  20.4 8.2 %all-to-all-done = bf16[8,14,1536]{2,1,0:T(8,128)(2,1)S(1)} async-done(((bf16[8,14,1536]{2,1,0:T(8,128)(2,1)}), bf16[8,14,1536]{2,1,0:T(8,128)(2,1)S(1)}, u32[]{:S(2)}, u32[]{:S(2)}) %all-to-all-start) | async-done | bytes 344096 | tf_op jit(solution)/shard_map/all_to_all | solution.py:85
  28.8 2.9 %collective-permute-start.2 = (bf16[56,3072]{1,0:T(8,128)(2,1)S(1)}, bf16[56,3072]{1,0:T(8,128)(2,1)S(1)}, u32[]{:S(2)}, u32[]{:S(2)}) collective-permute-start(bf16[56,3072]{1,0:T(8,128)(2,1)S(1)} %constant_dynamic-update-slice_fusion), channel_id=1, source_target_pairs={{384,0},{385,1},{386,2},{387,3},{388,4},{389,5},{390,6},{391,7},{0... | collective-permute-start | bytes 1032200 | tf_op jit(solution)/shard_map/ppermute | solution.py:63
  31.7 2.6 %collective-permute-start.1 = (bf16[56,3072]{1,0:T(8,128)(2,1)S(1)}, bf16[56,3072]{1,0:T(8,128)(2,1)S(1)}, u32[]{:S(2)}, u32[]{:S(2)}) collective-permute-start(bf16[56,3072]{1,0:T(8,128)(2,1)S(1)} %constant_dynamic-update-slice_fusion), channel_id=1, source_target_pairs={{256,0},{257,1},{258,2},{259,3},{260,4},{261,5},{262,6},{263,7},{3... | collective-permute-start | bytes 1032200 | tf_op jit(solution)/shard_map/ppermute | solution.py:63
  34.3 3.1 %collective-permute-start = (bf16[56,3072]{1,0:T(8,128)(2,1)S(1)}, bf16[56,3072]{1,0:T(8,128)(2,1)S(1)}, u32[]{:S(2)}, u32[]{:S(2)}) collective-permute-start(bf16[56,3072]{1,0:T(8,128)(2,1)S(1)} %constant_dynamic-update-slice_fusion), channel_id=1, source_target_pairs={{128,0},{129,1},{130,2},{131,3},{132,4},{133,5},{134,6},{135,7},{2... | collective-permute-start | bytes 1032200 | tf_op jit(solution)/shard_map/ppermute | solution.py:63
  37.4 1.1 collective-permute-done.2
  38.4 5.1 %collective-permute-done.1 = bf16[56,3072]{1,0:T(8,128)(2,1)S(1)} collective-permute-done((bf16[56,3072]{1,0:T(8,128)(2,1)S(1)}, bf16[56,3072]{1,0:T(8,128)(2,1)S(1)}, u32[]{:S(2)}, u32[]{:S(2)}) %collective-permute-start.1) | collective-permute-done | bytes 344096 | tf_op jit(solution)/shard_map/ppermute | solution.py:63
  43.5 4.8 %collective-permute-done = bf16[56,3072]{1,0:T(8,128)(2,1)S(1)} collective-permute-done((bf16[56,3072]{1,0:T(8,128)(2,1)S(1)}, bf16[56,3072]{1,0:T(8,128)(2,1)S(1)}, u32[]{:S(2)}, u32[]{:S(2)}) %collective-permute-start) | collective-permute-done | bytes 344096 | tf_op jit(solution)/shard_map/ppermute | solution.py:63
  48.4 2.0 %pad_maximum_fusion = bf16[1536,768]{1,0:T(8,128)(2,1)S(1)} fusion(bf16[1536,384]{1,0:T(8,128)(2,1)} %collective-permute-done.3, bf16[1536,384]{1,0:T(8,128)(2,1)S(1)} %copy-done.2), kind=kLoop, calls=%fused_computation.5 | loop fusion | flops 4718592 | bytes 4718592 | tf_op jit(solution)/shard_map/concatenate | solution.py:92
  50.7 0.9 fusion.7
  52.3 1.2 pad_maximum_fusion.3
  53.8 1.5 %multiply_convert_fusion = f16[4,56,1536]{2,1,0:T(8,128)(2,1)S(1)} fusion(f32[4,56,1536]{2,1,0:T(8,128)} %bitcast.8, f32[1536]{0:T(1024)S(1)} %exp2.58), kind=kLoop, calls=%fused_computation.10 | loop fusion | flops 688128 | bytes 2070528 | tf_op jit(solution)/shard_map/convert_element_type | solution.py:36
  55.5 12.9 %all_to_all.20 = f16[4,64,1536]{2,1,0:T(8,128)(2,1)S(1)} all-to-all(f16[4,64,1536]{2,1,0:T(8,128)(2,1)S(1)} %pad_maximum_fusion.4), channel_id=1, replica_groups={{0,16,32,48},{8,24,40,56},{1,17,33,49},{9,25,41,57},{2,18,34,50},{10,26..., dimensions={0} | all-to-all | bytes 1572864 | tf_op jit(solution)/shard_map/all_to_all | solution.py:104
  69.1 4.7 %collective-permute-start.5 = (f16[64,1536]{1,0:T(8,128)(2,1)S(1)}, f16[64,1536]{1,0:T(8,128)(2,1)S(1)}, u32[]{:S(2)}, u32[]{:S(2)}) collective-permute-start(f16[64,1536]{1,0:T(8,128)(2,1)S(1)} %pad_maximum_fusion.6), channel_id=1, source_target_pairs={{0,8},{8,0},{16,24},{24,16},{32,40},{40,32},{48,56},{56,48},{1,9},... | collective-permute-start | bytes 589832 | tf_op jit(solution)/shard_map/ppermute | solution.py:106
  73.8 7.8 %collective-permute-done.5 = f16[64,1536]{1,0:T(8,128)(2,1)S(1)} collective-permute-done((f16[64,1536]{1,0:T(8,128)(2,1)S(1)}, f16[64,1536]{1,0:T(8,128)(2,1)S(1)}, u32[]{:S(2)}, u32[]{:S(2)}) %collective-permute-start.5) | collective-permute-done | bytes 196640 | tf_op jit(solution)/shard_map/ppermute | solution.py:106
  81.8 0.9 broadcast_in_dim.37
  82.7 3.5 %all-to-all-start.2 = ((bf16[4,56,1536]{2,1,0:T(8,128)(2,1)}), bf16[4,56,1536]{2,1,0:T(8,128)(2,1)S(1)}, u32[]{:S(2)}, u32[]{:S(2)}) async-start(bf16[4,56,1536]{2,1,0:T(8,128)(2,1)} %broadcast_in_dim.37), calls=%async_computation.2 | async-start | bytes 1376256 | tf_op jit(solution)/shard_map/all_to_all | solution.py:111
  86.2 5.1 %collective-permute-start.9 = (bf16[224,3072]{1,0:T(8,128)(2,1)}, bf16[224,3072]{1,0:T(8,128)(2,1)}, u32[]{:S(2)}, u32[]{:S(2)}) collective-permute-start(bf16[224,3072]{1,0:T(8,128)(2,1)} %copy-done), channel_id=1, source_target_pairs={{0,64},{64,0},{128,192},{192,128},{256,320},{320,256},{384,448},{4... | collective-permute-start | bytes 4128776 | tf_op jit(solution)/shard_map/ppermute | solution.py:78
  91.3 2.8 %all-to-all-done.2 = bf16[4,56,1536]{2,1,0:T(8,128)(2,1)S(1)} async-done(((bf16[4,56,1536]{2,1,0:T(8,128)(2,1)}), bf16[4,56,1536]{2,1,0:T(8,128)(2,1)S(1)}, u32[]{:S(2)}, u32[]{:S(2)}) %all-to-all-start.2) | async-done | bytes 688160 | tf_op jit(solution)/shard_map/all_to_all | solution.py:111
  94.1 0.9 convolution_convert_fusion
  95.0 9.4 %collective-permute-start.6 = (bf16[56,1536]{1,0:T(8,128)(2,1)S(1)}, bf16[56,1536]{1,0:T(8,128)(2,1)S(1)}, u32[]{:S(2)}, u32[]{:S(2)}) collective-permute-start(bf16[56,1536]{1,0:T(8,128)(2,1)S(1)} %get-tuple-element.13), channel_id=1, source_target_pairs={{0,256},{1,257},{2,258},{3,259},{4,260},{5,261},{6,262},{7,263},{1... | collective-permute-start | bytes 516104 | tf_op jit(solution)/shard_map/ppermute | solution.py:66
  104.5 1.9 %collective-permute-start.8 = (bf16[56,1536]{1,0:T(8,128)(2,1)S(1)}, bf16[56,1536]{1,0:T(8,128)(2,1)S(1)}, u32[]{:S(2)}, u32[]{:S(2)}) collective-permute-start(bf16[56,1536]{1,0:T(8,128)(2,1)S(1)} %get-tuple-element.14), channel_id=1, source_target_pairs={{0,384},{1,385},{2,386},{3,387},{4,388},{5,389},{6,390},{7,391},{1... | collective-permute-start | bytes 516104 | tf_op jit(solution)/shard_map/ppermute | solution.py:66
  106.4 3.4 %collective-permute-start.7 = (bf16[56,1536]{1,0:T(8,128)(2,1)S(1)}, bf16[56,1536]{1,0:T(8,128)(2,1)S(1)}, u32[]{:S(2)}, u32[]{:S(2)}) collective-permute-start(bf16[56,1536]{1,0:T(8,128)(2,1)S(1)} %get-tuple-element.15), channel_id=1, source_target_pairs={{0,128},{1,129},{2,130},{3,131},{4,132},{5,133},{6,134},{7,135},{1... | collective-permute-start | bytes 516104 | tf_op jit(solution)/shard_map/ppermute | solution.py:66
  109.8 3.3 %collective-permute-start.10 = (bf16[224,768]{1,0:T(8,128)(2,1)S(1)}, bf16[224,768]{1,0:T(8,128)(2,1)S(1)}, u32[]{:S(2)}, u32[]{:S(2)}) collective-permute-start(bf16[224,768]{1,0:T(8,128)(2,1)S(1)} %pad_maximum_fusion.5), channel_id=1, source_target_pairs={{0,64},{64,0},{128,192},{192,128},{256,320},{320,256},{384,448},{4... | collective-permute-start | bytes 1032200 | tf_op jit(solution)/shard_map/ppermute | solution.py:78
  114.6 6.2 %all-to-all-start.3 = ((bf16[8,7,1536]{2,1,0:T(8,128)(2,1)}), bf16[8,7,1536]{2,1,0:T(8,128)(2,1)S(1)}, u32[]{:S(2)}, u32[]{:S(2)}) async-start(bf16[8,7,1536]{2,1,0:T(8,128)(2,1)} %reshape.67), calls=%async_computation.3 | async-start | bytes 393216 | tf_op jit(solution)/shard_map/all_to_all | solution.py:126
  120.9 1.7 %fusion.2 = f32[384,1536]{1,0:T(8,128)S(1)} fusion(bf16[224,3072]{1,0:T(8,128)(2,1)} %collective-permute-done.9, bf16[224,768]{1,0:T(8,128)(2,1)S(1)} %collective-permute-done.10), kind=kOutput, calls=%fused_computation.13 | convolution fusion | flops 264241152 | bytes 3219456 | tf_op jit(solution)/shard_map/dot_general | solution.py:27
  122.6 1.5 %fusion.1 = bf16[384,1536]{1,0:T(8,128)(2,1)} fusion(f32[384,1536]{1,0:T(8,128)S(1)} %fusion.2, bf16[224,3072]{1,0:T(8,128)(2,1)S(1)} %copy-done.1, bf16[224,1536]{1,0:T(8,128)(2,1)S(1)} %bitcast.11), kind=kOutput, calls=%fused_computation.3 | convolution fusion | flops 265420800 | bytes 4399104 | tf_op jit(solution)/shard_map/dot_general | solution.py:27
  124.1 1.7 %fusion.4 = f32[1536,384]{1,0:T(8,128)S(1)} fusion(bf16[224,3072]{1,0:T(8,128)(2,1)} %collective-permute-done.9, bf16[224,768]{1,0:T(8,128)(2,1)S(1)} %collective-permute-done.10), kind=kOutput, calls=%fused_computation.15 | convolution fusion | flops 264241152 | bytes 3219456 | tf_op jit(solution)/shard_map/dot_general | solution.py:27
  125.8 1.6 %fusion = bf16[1536,384]{1,0:T(8,128)(2,1)} fusion(f32[1536,384]{1,0:T(8,128)S(1)} %fusion.4, bf16[224,3072]{1,0:T(8,128)(2,1)S(1)} %copy-done.1, bf16[224,1536]{1,0:T(8,128)(2,1)S(1)} %bitcast.12), kind=kOutput, calls=%fused_computation.2 | convolution fusion | flops 265420800 | bytes 4399104 | tf_op jit(solution)/shard_map/dot_general | solution.py:27
  127.5 4.0 %all-to-all-done.3 = bf16[8,7,1536]{2,1,0:T(8,128)(2,1)S(1)} async-done(((bf16[8,7,1536]{2,1,0:T(8,128)(2,1)}), bf16[8,7,1536]{2,1,0:T(8,128)(2,1)S(1)}, u32[]{:S(2)}, u32[]{:S(2)}) %all-to-all-start.3) | async-done | bytes 172064 | tf_op jit(solution)/shard_map/all_to_all | solution.py:126
  (58 shorter events, 6.5 us)
Async XLA Ops:
  2.2 26.4 %all-to-all-start = ((bf16[8,14,1536]{2,1,0:T(8,128)(2,1)}), bf16[8,14,1536]{2,1,0:T(8,128)(2,1)S(1)}, u32[]{:S(2)}, u32[]{:S(2)}) async-start(bf16[8,14,1536]{2,1,0:T(8,128)(2,1)} %broadcast_in_dim.30), calls=%async_computation | async-start | bytes 786432 | tf_op jit(solution)/shard_map/all_to_all | solution.py:85
  16.1 32.4 %collective-permute-start.3 = (bf16[1536,384]{1,0:T(8,128)(2,1)}, bf16[1536,384]{1,0:T(8,128)(2,1)}, u32[]{:S(2)}, u32[]{:S(2)}) collective-permute-start(bf16[1536,384]{1,0:T(8,128)(2,1)} %param.5), channel_id=1, source_target_pairs={{0,64},{64,0},{128,192},{192,128},{256,320},{320,256},{384,448},{4... | collective-permute-start | bytes 3538952 | tf_op jit(solution)/shard_map/ppermute | solution.py:78
  18.0 32.5 %collective-permute-start.4 = (bf16[384,1536]{1,0:T(8,128)(2,1)}, bf16[384,1536]{1,0:T(8,128)(2,1)S(1)}, u32[]{:S(2)}, u32[]{:S(2)}) collective-permute-start(bf16[384,1536]{1,0:T(8,128)(2,1)} %param.6), channel_id=1, source_target_pairs={{0,64},{64,0},{128,192},{192,128},{256,320},{320,256},{384,448},{4... | collective-permute-start | bytes 3538952 | tf_op jit(solution)/shard_map/ppermute | solution.py:78
  28.8 19.6 %copy-start.2 = (bf16[1536,384]{1,0:T(8,128)(2,1)S(1)}, bf16[1536,384]{1,0:T(8,128)(2,1)}, u32[]{:S(2)}) copy-start(bf16[1536,384]{1,0:T(8,128)(2,1)} %param.5) | copy-start | bytes 3538948
  28.8 9.6 %collective-permute-start.2 = (bf16[56,3072]{1,0:T(8,128)(2,1)S(1)}, bf16[56,3072]{1,0:T(8,128)(2,1)S(1)}, u32[]{:S(2)}, u32[]{:S(2)}) collective-permute-start(bf16[56,3072]{1,0:T(8,128)(2,1)S(1)} %constant_dynamic-update-slice_fusion), channel_id=1, source_target_pairs={{384,0},{385,1},{386,2},{387,3},{388,4},{389,5},{390,6},{391,7},{0... | collective-permute-start | bytes 1032200 | tf_op jit(solution)/shard_map/ppermute | solution.py:63
  31.7 11.8 %collective-permute-start.1 = (bf16[56,3072]{1,0:T(8,128)(2,1)S(1)}, bf16[56,3072]{1,0:T(8,128)(2,1)S(1)}, u32[]{:S(2)}, u32[]{:S(2)}) collective-permute-start(bf16[56,3072]{1,0:T(8,128)(2,1)S(1)} %constant_dynamic-update-slice_fusion), channel_id=1, source_target_pairs={{256,0},{257,1},{258,2},{259,3},{260,4},{261,5},{262,6},{263,7},{3... | collective-permute-start | bytes 1032200 | tf_op jit(solution)/shard_map/ppermute | solution.py:63
  34.3 14.0 %collective-permute-start = (bf16[56,3072]{1,0:T(8,128)(2,1)S(1)}, bf16[56,3072]{1,0:T(8,128)(2,1)S(1)}, u32[]{:S(2)}, u32[]{:S(2)}) collective-permute-start(bf16[56,3072]{1,0:T(8,128)(2,1)S(1)} %constant_dynamic-update-slice_fusion), channel_id=1, source_target_pairs={{128,0},{129,1},{130,2},{131,3},{132,4},{133,5},{134,6},{135,7},{2... | collective-permute-start | bytes 1032200 | tf_op jit(solution)/shard_map/ppermute | solution.py:63
  48.4 3.2 %copy-start = (bf16[224,3072]{1,0:T(8,128)(2,1)}, bf16[224,3072]{1,0:T(8,128)(2,1)S(1)}, u32[]{:S(2)}) copy-start(bf16[224,3072]{1,0:T(8,128)(2,1)S(1)} %pad_maximum_fusion.2) | copy-start | bytes 4128772
  48.4 2.1 %copy-start.3 = (bf16[384,1536]{1,0:T(8,128)(2,1)S(1)}, bf16[384,1536]{1,0:T(8,128)(2,1)}, u32[]{:S(2)}) copy-start(bf16[384,1536]{1,0:T(8,128)(2,1)} %param.6) | copy-start | bytes 3538948
  69.1 12.5 %collective-permute-start.5 = (f16[64,1536]{1,0:T(8,128)(2,1)S(1)}, f16[64,1536]{1,0:T(8,128)(2,1)S(1)}, u32[]{:S(2)}, u32[]{:S(2)}) collective-permute-start(f16[64,1536]{1,0:T(8,128)(2,1)S(1)} %pad_maximum_fusion.6), channel_id=1, source_target_pairs={{0,8},{8,0},{16,24},{24,16},{32,40},{40,32},{48,56},{56,48},{1,9},... | collective-permute-start | bytes 589832 | tf_op jit(solution)/shard_map/ppermute | solution.py:106
  82.7 11.3 %all-to-all-start.2 = ((bf16[4,56,1536]{2,1,0:T(8,128)(2,1)}), bf16[4,56,1536]{2,1,0:T(8,128)(2,1)S(1)}, u32[]{:S(2)}, u32[]{:S(2)}) async-start(bf16[4,56,1536]{2,1,0:T(8,128)(2,1)} %broadcast_in_dim.37), calls=%async_computation.2 | async-start | bytes 1376256 | tf_op jit(solution)/shard_map/all_to_all | solution.py:111
  86.2 34.6 %collective-permute-start.9 = (bf16[224,3072]{1,0:T(8,128)(2,1)}, bf16[224,3072]{1,0:T(8,128)(2,1)}, u32[]{:S(2)}, u32[]{:S(2)}) collective-permute-start(bf16[224,3072]{1,0:T(8,128)(2,1)} %copy-done), channel_id=1, source_target_pairs={{0,64},{64,0},{128,192},{192,128},{256,320},{320,256},{384,448},{4... | collective-permute-start | bytes 4128776 | tf_op jit(solution)/shard_map/ppermute | solution.py:78
  95.0 18.0 %collective-permute-start.6 = (bf16[56,1536]{1,0:T(8,128)(2,1)S(1)}, bf16[56,1536]{1,0:T(8,128)(2,1)S(1)}, u32[]{:S(2)}, u32[]{:S(2)}) collective-permute-start(bf16[56,1536]{1,0:T(8,128)(2,1)S(1)} %get-tuple-element.13), channel_id=1, source_target_pairs={{0,256},{1,257},{2,258},{3,259},{4,260},{5,261},{6,262},{7,263},{1... | collective-permute-start | bytes 516104 | tf_op jit(solution)/shard_map/ppermute | solution.py:66
  104.5 8.6 %collective-permute-start.8 = (bf16[56,1536]{1,0:T(8,128)(2,1)S(1)}, bf16[56,1536]{1,0:T(8,128)(2,1)S(1)}, u32[]{:S(2)}, u32[]{:S(2)}) collective-permute-start(bf16[56,1536]{1,0:T(8,128)(2,1)S(1)} %get-tuple-element.14), channel_id=1, source_target_pairs={{0,384},{1,385},{2,386},{3,387},{4,388},{5,389},{6,390},{7,391},{1... | collective-permute-start | bytes 516104 | tf_op jit(solution)/shard_map/ppermute | solution.py:66
  106.4 7.4 %collective-permute-start.7 = (bf16[56,1536]{1,0:T(8,128)(2,1)S(1)}, bf16[56,1536]{1,0:T(8,128)(2,1)S(1)}, u32[]{:S(2)}, u32[]{:S(2)}) collective-permute-start(bf16[56,1536]{1,0:T(8,128)(2,1)S(1)} %get-tuple-element.15), channel_id=1, source_target_pairs={{0,128},{1,129},{2,130},{3,131},{4,132},{5,133},{6,134},{7,135},{1... | collective-permute-start | bytes 516104 | tf_op jit(solution)/shard_map/ppermute | solution.py:66
  109.8 11.1 %collective-permute-start.10 = (bf16[224,768]{1,0:T(8,128)(2,1)S(1)}, bf16[224,768]{1,0:T(8,128)(2,1)S(1)}, u32[]{:S(2)}, u32[]{:S(2)}) collective-permute-start(bf16[224,768]{1,0:T(8,128)(2,1)S(1)} %pad_maximum_fusion.5), channel_id=1, source_target_pairs={{0,64},{64,0},{128,192},{192,128},{256,320},{320,256},{384,448},{4... | collective-permute-start | bytes 1032200 | tf_op jit(solution)/shard_map/ppermute | solution.py:78
  114.6 16.8 %all-to-all-start.3 = ((bf16[8,7,1536]{2,1,0:T(8,128)(2,1)}), bf16[8,7,1536]{2,1,0:T(8,128)(2,1)S(1)}, u32[]{:S(2)}, u32[]{:S(2)}) async-start(bf16[8,7,1536]{2,1,0:T(8,128)(2,1)} %reshape.67), calls=%async_computation.3 | async-start | bytes 393216 | tf_op jit(solution)/shard_map/all_to_all | solution.py:126
  120.8 1.7 %copy-start.1 = (bf16[224,3072]{1,0:T(8,128)(2,1)S(1)}, bf16[224,3072]{1,0:T(8,128)(2,1)}, u32[]{:S(2)}) copy-start(bf16[224,3072]{1,0:T(8,128)(2,1)} %copy-done) | copy-start | bytes 4128772

commit v4 on v3

--- a/solution.py
+++ b/solution.py
@@ -1,11 +1,12 @@
 import jax
 import jax.numpy as jnp
 from jax import lax
+from jax.experimental import pallas as pl
+from jax.experimental.pallas import tpu as pltpu
 from jax.sharding import PartitionSpec as P
 
 coeff = 0.7978845608
 bf16 = jnp.bfloat16
-f16 = jnp.float16
 f32 = jnp.float32
 
 
@@ -27,18 +28,57 @@
     return lax.dot_general(left, right, (((0,), (0,)), ((), ())), preferred_element_type=f32)
 
 
-def pack(sums):
-    columns = sums.shape[-1]
-    kinds = sums.reshape(-1, 2, columns // 2)
-    most = jnp.maximum(jnp.max(jnp.abs(kinds), axis=(0, 2)), 1e-30)
-    power = jnp.repeat(jnp.round(jnp.log2(most)), columns // 2)
-    tail = jnp.broadcast_to(power, (*sums.shape[:-2], 8, columns))
-    return jnp.concatenate([(sums * jnp.exp2(13.0 - power)).astype(f16), tail.astype(f16)], axis=-2)
-
-
-def unpack(packed):
-    power = packed[..., -8:-7, :].astype(f32)
-    return packed[..., :-8, :].astype(f32) * jnp.exp2(power - 13.0)
+def first_products(
+    own_ref, in0, in1, out0, out1, parts_ref, mine_ref, kept_in, kept_grad, held_in, held_out, total, sems
+):
+    width, hidden = in0.shape
+    blocks, share, _ = parts_ref.shape
+    copies = [
+        pltpu.make_async_copy(in0, held_in.at[:, :hidden], sems.at[0]),
+        pltpu.make_async_copy(in1, held_in.at[:, hidden:], sems.at[1]),
+        pltpu.make_async_copy(out0, held_out.at[:hidden], sems.at[2]),
+        pltpu.make_async_copy(out1, held_out.at[hidden:], sems.at[3]),
+        pltpu.make_async_copy(own_ref.at[:, :width], kept_in, sems.at[4]),
+        pltpu.make_async_copy(own_ref.at[:, width:], kept_grad, sems.at[5]),
+    ]
+    for copy in copies:
+        copy.start()
+
+    def put(product, columns):
+        total[:, columns] = product
+        for b in range(blocks):
+            parts_ref[b, :, columns] = product[b * share : (b + 1) * share].astype(bf16)
+
+    copies[0].wait()
+    copies[1].wait()
+    put(jnp.dot(own_ref[:, :width], held_in[...], preferred_element_type=f32), slice(0, 2 * hidden))
+    copies[2].wait()
+    copies[3].wait()
+    put(contract_last(own_ref[:, width:], held_out[...]), slice(2 * hidden, 4 * hidden))
+    block = lax.div(lax.axis_index("gy"), lax.div(lax.axis_size("gy"), blocks))
+    mine_ref[...] = total[pl.ds(pl.multiple_of(block * share, share), share), :]
+    parts_ref[block] = jnp.zeros((share, 4 * hidden), bf16)
+    copies[4].wait()
+    copies[5].wait()
+
+
+def last_product(whole_ref, in0, in1, rounded_ref, mine_ref, other_ref, held, sems):
+    width, hidden = in0.shape
+    blocks, share, _ = rounded_ref.shape
+    copies = [
+        pltpu.make_async_copy(in0, held.at[:, :hidden], sems.at[0]),
+        pltpu.make_async_copy(in1, held.at[:, hidden:], sems.at[1]),
+    ]
+    for copy in copies:
+        copy.start()
+    other_ref[:, :hidden] = whole_ref[:, hidden : 2 * hidden]
+    other_ref[:, hidden:] = whole_ref[:, 3 * hidden :]
+    for copy in copies:
+        copy.wait()
+    product = contract_last(whole_ref[:, 2 * hidden :], held[...])
+    for b in range(blocks):
+        rounded_ref[b] = product[b * share : (b + 1) * share].astype(bf16)
+    mine_ref[...] = product[:share]
 
 
 class Routes:
@@ -89,49 +129,75 @@
     near = jnp.concatenate(
         [near[:, :rows].reshape(share, width), near[:, rows:].reshape(share, width)], axis=1
     )
-    chip_in = jnp.concatenate([weight_in, swap(weight_in)], axis=1)
-    chip_out = jnp.concatenate([weight_out, swap(weight_out)], axis=0)
-    chip_in, chip_out = lax.optimization_barrier((chip_in, chip_out))
+    other_in, other_out = swap(weight_in), swap(weight_out)
     found = routes.send(near, ("gx", "gz"))
-    own = jnp.concatenate([near] + [found[b] for b in range(1, blocks)], axis=0)
-    own_in, own_grad = own[:, :width], own[:, width:]
-    swapped = swap(own)
+    found = [near] + [found[b] for b in range(1, blocks)]
+    own = jnp.concatenate(found, axis=0)
     tokens = blocks * share
 
-    pre_part = jnp.dot(own_in, chip_in, preferred_element_type=f32)
-    dact_part = contract_last(own_grad, chip_out)
-    parts = pack(jnp.concatenate([pre_part, dact_part], axis=1).reshape(blocks, share, 4 * hidden))
+    vmem, anywhere = pl.BlockSpec(memory_space=pltpu.VMEM), pl.BlockSpec(memory_space=pl.ANY)
+    mib = 1024 * 1024
+    parts, mine, kept_in, kept_grad = pl.pallas_call(
+        first_products,
+        out_shape=(
+            jax.ShapeDtypeStruct((blocks, share, 4 * hidden), bf16),
+            jax.ShapeDtypeStruct((share, 4 * hidden), f32),
+            jax.ShapeDtypeStruct((tokens, width), bf16),
+            jax.ShapeDtypeStruct((tokens, width), bf16),
+        ),
+        in_specs=[vmem] + [anywhere] * 4,
+        out_specs=(vmem, vmem, anywhere, anywhere),
+        scratch_shapes=[
+            pltpu.VMEM((width, 2 * hidden), bf16),
+            pltpu.VMEM((2 * hidden, width), bf16),
+            pltpu.VMEM((tokens, 4 * hidden), f32),
+            pltpu.SemaphoreType.DMA((6,)),
+        ],
+        compiler_params=pltpu.CompilerParams(vmem_limit_bytes=14 * mib),
+        cost_estimate=pl.CostEstimate(
+            flops=8 * tokens * width * hidden, bytes_accessed=8 * width * hidden, transcendentals=0
+        ),
+    )(own, weight_in, other_in, weight_out, other_out)
+    swapped_in, swapped_grad = swap(kept_in), swap(kept_grad)
     parts = lax.all_to_all(parts, "gy", 0, 0, axis_index_groups=same_half)
-    sums = jnp.sum(unpack(parts), axis=0)
-    sums = sums + unpack(lax.ppermute(pack(sums), "gy", other_half))
+    sums = mine + jnp.sum(parts.astype(f32), axis=0)
+    sums = sums + lax.ppermute(sums.astype(bf16), "gy", other_half).astype(f32)
     pre, dact = sums[:, : 2 * hidden], sums[:, 2 * hidden :]
     act = gelu_value(pre).astype(bf16)
     dpre = (dact * gelu_slope(pre)).astype(bf16)
-    mine = jnp.concatenate([act, dpre], axis=1)
+    done = jnp.concatenate([act, dpre], axis=1)
     whole = lax.all_to_all(
-        jnp.broadcast_to(mine[None], (blocks, share, 4 * hidden)), "gy", 0, 0, axis_index_groups=same_half
+        jnp.broadcast_to(done[None], (blocks, share, 4 * hidden)), "gy", 0, 0, axis_index_groups=same_half
     ).reshape(tokens, 4 * hidden)
-    act_own, act_other = whole[:, :hidden], whole[:, hidden : 2 * hidden]
-    dpre_own, dpre_other = whole[:, 2 * hidden : 3 * hidden], whole[:, 3 * hidden :]
-
-    chip_sum = contract_last(whole[:, 2 * hidden :], chip_in).astype(bf16)
-    for_other, chip_sum = lax.optimization_barrier(
-        (jnp.concatenate([act_other, dpre_other], axis=1), chip_sum)
-    )
-    chip_sum = chip_sum.reshape(blocks, share, width)
-    total = chip_sum[0].astype(f32)
-    for v in routes.send_back(chip_sum, ("gx", "gz")):
+    rounded, total, for_other = pl.pallas_call(
+        last_product,
+        out_shape=(
+            jax.ShapeDtypeStruct((blocks, share, width), bf16),
+            jax.ShapeDtypeStruct((share, width), f32),
+            jax.ShapeDtypeStruct((tokens, 2 * hidden), bf16),
+        ),
+        in_specs=[vmem, anywhere, anywhere],
+        out_specs=(vmem, vmem, vmem),
+        scratch_shapes=[pltpu.VMEM((width, 2 * hidden), bf16), pltpu.SemaphoreType.DMA((2,))],
+        compiler_params=pltpu.CompilerParams(vmem_limit_bytes=10 * mib),
+        cost_estimate=pl.CostEstimate(
+            flops=4 * tokens * width * hidden, bytes_accessed=4 * width * hidden, transcendentals=0
+        ),
+    )(whole, weight_in, other_in)
+    for v in routes.send_back(rounded, ("gx", "gz")):
         total = total + v.astype(f32)
     swapped_whole = swap(for_other)
     pieces = lax.all_to_all(
         total.astype(bf16).reshape(nz, rows, width), ("gx", "gz"), 0, 0, axis_index_groups=routes.first
     )
     grad_inputs = jnp.sum(pieces.astype(f32), axis=0).astype(bf16)
-    grad_weight_out = (
-        contract_first(act_own, own_grad) + contract_first(swapped_whole[:, :hidden], swapped[:, width:])
+    grad_weight_out = contract_first(
+        jnp.concatenate([whole[:, :hidden], swapped_whole[:, :hidden]], axis=0),
+        jnp.concatenate([kept_grad, swapped_grad], axis=0),
     ).astype(bf16)
-    grad_weight_in = (
-        contract_first(own_in, dpre_own) + contract_first(swapped[:, :width], swapped_whole[:, hidden:])
+    grad_weight_in = contract_first(
+        jnp.concatenate([kept_in, swapped_in], axis=0),
+        jnp.concatenate([whole[:, 2 * hidden : 3 * hidden], swapped_whole[:, hidden:]], axis=0),
     ).astype(bf16)
     return (grad_inputs, grad_weight_in, grad_weight_out)
 

time: 133 us -> 127 us (0.955)
  other arithmetic: 7.43 us -> 1.92 us
  starting transfers between devices: 64.2 us -> 68.4 us
  waiting for transfers between devices: 34.3 us -> 30.3 us
  Pallas kernels: 0 us -> 3.99 us
  matrix products: 9 us -> 6.12 us
    ppermute x4 -> x5, starting transfers between devices: 12.7 us -> 19.7 us  [swap(): return lax.ppermute(v, 'gx', swap_cores)]
    pallas_call x0 -> x2, Pallas kernels: none -> 3.99 us  [the longest x1 2.83 us: per_device(): pl.pallas_call(first_products, out_shape=(jax.ShapeDtypeStruct((blocks, s...]
    concatenate x8 -> x2, other arithmetic: 3.69 us -> 0.1 us  [the longest x1 0.09 us: per_device(): own = jnp.concatenate(found, axis=0)]
    ppermute x3, starting transfers between devices: 14.7 us -> 11.5 us  [send_back(): lax.ppermute(sources[b], axes, [(d, s) for s, d in pairs])]
    all_to_all x1, waiting for transfers between devices: 2.75 us -> 0.01 us  [per_device(): lax.all_to_all(jnp.broadcast_to(done[None], (blocks, share, 4 * hidden)),...]
    dot_general x3 -> x0, matrix products: 2.43 us -> none  [the longest x2 1.74 us: contract_last(): lax.dot_general(left, right, (((1,), (1,)), ((), ())), preferred_element_...]
    convert_element_type x2 -> x1, other arithmetic: 1.5 us -> 0.05 us  [per_device(): sums = sums + lax.ppermute(sums.astype(bf16), 'gy', other_half).astype(f32)]
    dot_general x4 -> x2, matrix products: 6.57 us -> 6.12 us  [contract_first(): lax.dot_general(left, right, (((0,), (0,)), ((), ())), preferred_element_...]
  transfers between devices with their start and end apart: 14 -> 15, of which waited for: 8 -> 6; matrix products, arithmetic and copies ran while one was open for 8% -> 6% of each run, Pallas kernels for 0% -> 1%
where the time goes in v4:
time: 127 us; the launch traced here: 126 us
  starting transfers between devices  68.4 us (54%)
  waiting for transfers between devices  30.3 us (24%)
  blocking collectives  11.6 us (9%)
  matrix products  6.12 us (5%)
  Pallas kernels  3.99 us (3%)
  local copies, waits for them, and re-layouts  2.77 us (2%)
  other arithmetic  1.92 us (2%)
    ppermute x5, starting transfers between devices, swap(): return lax.ppermute(v, 'gx', swap_cores)  19.7 us
    all_to_all x1, starting transfers between devices, per_device(): lax.all_to_all(jnp.broadcast_to(both[None], (nz, 2 * rows, width)), ('gx'...  13.9 us
    all_to_all x1, blocking collectives, per_device(): parts = lax.all_to_all(parts, 'gy', 0, 0, axis_index_groups=same_half)  11.6 us
    ppermute x3, starting transfers between devices, send_back(): lax.ppermute(sources[b], axes, [(d, s) for s, d in pairs])  11.5 us
    ppermute x3, waiting for transfers between devices, send(): return {b: lax.ppermute(source, axes, pairs) for b, pairs in self.moves}  10.9 us
    ppermute x3, starting transfers between devices, send(): return {b: lax.ppermute(source, axes, pairs) for b, pairs in self.moves}  8.55 us
    all_to_all x1, waiting for transfers between devices, per_device(): lax.all_to_all(jnp.broadcast_to(both[None], (nz, 2 * rows, width)), ('gx'...  8.16 us
    ppermute x1, waiting for transfers between devices, per_device(): sums = sums + lax.ppermute(sums.astype(bf16), 'gy', other_half).astype(f32)  6.81 us
  transfers between devices with their start and end apart: 15, of which 6 were waited for; matrix products, arithmetic and copies ran while one was open for 6% of the time, Pallas kernels for 1%

profile of v4, /device:TPU:1, one launch (start us, length us, event | category | flops | bytes accessed | tf_op | source)
XLA Modules:
  0.0 126.1 jit_solution(5711618248269776362)
XLA Ops:
  0.6 0.8 pad_maximum_fusion.2
  1.4 0.8 broadcast_in_dim.4
  2.2 13.9 %all-to-all-start = ((bf16[8,14,1536]{2,1,0:T(8,128)(2,1)}), bf16[8,14,1536]{2,1,0:T(8,128)(2,1)S(1)}, u32[]{:S(2)}, u32[]{:S(2)}) async-start(bf16[8,14,1536]{2,1,0:T(8,128)(2,1)} %broadcast_in_dim.4), calls=%async_computation | async-start | bytes 786432 | tf_op jit(solution)/shard_map/all_to_all | solution.py:125
  16.1 1.9 %collective-permute-start.4 = (bf16[384,1536]{1,0:T(8,128)(2,1)}, bf16[384,1536]{1,0:T(8,128)(2,1)S(1)}, u32[]{:S(2)}, u32[]{:S(2)}) collective-permute-start(bf16[384,1536]{1,0:T(8,128)(2,1)} %out0.1), channel_id=1, source_target_pairs={{0,64},{64,0},{128,192},{192,128},{256,320},{320,256},{384,448},{4... | collective-permute-start | bytes 3538952 | tf_op jit(solution)/shard_map/ppermute | solution.py:118
  18.0 2.4 %collective-permute-start.3 = (bf16[1536,384]{1,0:T(8,128)(2,1)}, bf16[1536,384]{1,0:T(8,128)(2,1)S(1)}, u32[]{:S(2)}, u32[]{:S(2)}) collective-permute-start(bf16[1536,384]{1,0:T(8,128)(2,1)} %in0.3), channel_id=1, source_target_pairs={{0,64},{64,0},{128,192},{192,128},{256,320},{320,256},{384,448},{4... | collective-permute-start | bytes 3538952 | tf_op jit(solution)/shard_map/ppermute | solution.py:118
  20.4 8.2 %all-to-all-done = bf16[8,14,1536]{2,1,0:T(8,128)(2,1)S(1)} async-done(((bf16[8,14,1536]{2,1,0:T(8,128)(2,1)}), bf16[8,14,1536]{2,1,0:T(8,128)(2,1)S(1)}, u32[]{:S(2)}, u32[]{:S(2)}) %all-to-all-start) | async-done | bytes 344096 | tf_op jit(solution)/shard_map/all_to_all | solution.py:125
  28.8 2.9 %collective-permute-start.2 = (bf16[56,3072]{1,0:T(8,128)(2,1)S(1)}, bf16[56,3072]{1,0:T(8,128)(2,1)S(1)}, u32[]{:S(2)}, u32[]{:S(2)}) collective-permute-start(bf16[56,3072]{1,0:T(8,128)(2,1)S(1)} %constant_dynamic-update-slice_fusion), channel_id=1, source_target_pairs={{384,0},{385,1},{386,2},{387,3},{388,4},{389,5},{390,6},{391,7},{0... | collective-permute-start | bytes 1032200 | tf_op jit(solution)/shard_map/ppermute | solution.py:103
  31.7 2.6 %collective-permute-start.1 = (bf16[56,3072]{1,0:T(8,128)(2,1)S(1)}, bf16[56,3072]{1,0:T(8,128)(2,1)S(1)}, u32[]{:S(2)}, u32[]{:S(2)}) collective-permute-start(bf16[56,3072]{1,0:T(8,128)(2,1)S(1)} %constant_dynamic-update-slice_fusion), channel_id=1, source_target_pairs={{256,0},{257,1},{258,2},{259,3},{260,4},{261,5},{262,6},{263,7},{3... | collective-permute-start | bytes 1032200 | tf_op jit(solution)/shard_map/ppermute | solution.py:103
  34.3 3.1 %collective-permute-start = (bf16[56,3072]{1,0:T(8,128)(2,1)S(1)}, bf16[56,3072]{1,0:T(8,128)(2,1)S(1)}, u32[]{:S(2)}, u32[]{:S(2)}) collective-permute-start(bf16[56,3072]{1,0:T(8,128)(2,1)S(1)} %constant_dynamic-update-slice_fusion), channel_id=1, source_target_pairs={{128,0},{129,1},{130,2},{131,3},{132,4},{133,5},{134,6},{135,7},{2... | collective-permute-start | bytes 1032200 | tf_op jit(solution)/shard_map/ppermute | solution.py:103
  37.4 1.1 collective-permute-done.2
  38.5 5.1 %collective-permute-done.1 = bf16[56,3072]{1,0:T(8,128)(2,1)S(1)} collective-permute-done((bf16[56,3072]{1,0:T(8,128)(2,1)S(1)}, bf16[56,3072]{1,0:T(8,128)(2,1)S(1)}, u32[]{:S(2)}, u32[]{:S(2)}) %collective-permute-start.1) | collective-permute-done | bytes 344096 | tf_op jit(solution)/shard_map/ppermute | solution.py:103
  43.5 4.8 %collective-permute-done = bf16[56,3072]{1,0:T(8,128)(2,1)S(1)} collective-permute-done((bf16[56,3072]{1,0:T(8,128)(2,1)S(1)}, bf16[56,3072]{1,0:T(8,128)(2,1)S(1)}, u32[]{:S(2)}, u32[]{:S(2)}) %collective-permute-start) | collective-permute-done | bytes 344096 | tf_op jit(solution)/shard_map/ppermute | solution.py:103
  48.5 2.8 %shard_map.67 = (bf16[4,56,1536]{2,1,0:T(8,128)(2,1)S(1)}, f32[56,1536]{1,0:T(8,128)S(1)}, bf16[224,1536]{1,0:T(8,128)(2,1)S(1)}, bf16[224,1536]{1,0:T(8,128)(2,1)S(1)}) custom-call(bf16[224,3072]{1,0:T(8,128)(2,1)S(1)} %pad_maximum_fusion.own_ref, bf16[1536,384]{1,0:T(8,128)(2,1)S(1)} %copy-done, bf16[1536,384]{1,0:T(8,128)(2,1)S(1)} %collective-permute-done.3.in1, ...), custom_call_target="tpu_custom_call" | custom-call | flops 1056964608 | bytes 4718592 | tf_op jit(solution)/shard_map/pallas_call | solution.py:140
  51.3 11.6 %all_to_all.20 = bf16[4,56,1536]{2,1,0:T(8,128)(2,1)S(1)} all-to-all(bf16[4,56,1536]{2,1,0:T(8,128)(2,1)S(1)} %get-tuple-element.11), channel_id=1, replica_groups={{0,16,32,48},{8,24,40,56},{1,17,33,49},{9,25,41,57},{2,18,34,50},{10,26..., dimensions={0} | all-to-all | bytes 1376256 | tf_op jit(solution)/shard_map/all_to_all | solution.py:162
  63.1 4.7 %collective-permute-start.5 = (bf16[56,1536]{1,0:T(8,128)(2,1)S(1)}, bf16[56,1536]{1,0:T(8,128)(2,1)S(1)}, u32[]{:S(2)}, u32[]{:S(2)}) collective-permute-start(bf16[56,1536]{1,0:T(8,128)(2,1)S(1)} %get-tuple-element.17), channel_id=1, source_target_pairs={{0,8},{8,0},{16,24},{24,16},{32,40},{40,32},{48,56},{56,48},{1,9},... | collective-permute-start | bytes 516104 | tf_op jit(solution)/shard_map/ppermute | solution.py:164
  67.8 6.8 %collective-permute-done.5 = bf16[56,1536]{1,0:T(8,128)(2,1)S(1)} collective-permute-done((bf16[56,1536]{1,0:T(8,128)(2,1)S(1)}, bf16[56,1536]{1,0:T(8,128)(2,1)S(1)}, u32[]{:S(2)}, u32[]{:S(2)}) %collective-permute-start.5) | collective-permute-done | bytes 172064 | tf_op jit(solution)/shard_map/ppermute | solution.py:164
  74.7 0.1 multiply_convert_fusion
  74.8 0.9 broadcast_in_dim.5
  75.7 3.5 %all-to-all-start.2 = ((bf16[4,56,1536]{2,1,0:T(8,128)(2,1)}), bf16[4,56,1536]{2,1,0:T(8,128)(2,1)S(1)}, u32[]{:S(2)}, u32[]{:S(2)}) async-start(bf16[4,56,1536]{2,1,0:T(8,128)(2,1)} %broadcast_in_dim.5), calls=%async_computation.2 | async-start | bytes 1376256 | tf_op jit(solution)/shard_map/all_to_all | solution.py:169
  79.2 6.2 %collective-permute-start.9 = (bf16[224,1536]{1,0:T(8,128)(2,1)}, bf16[224,1536]{1,0:T(8,128)(2,1)}, u32[]{:S(2)}, u32[]{:S(2)}) collective-permute-start(bf16[224,1536]{1,0:T(8,128)(2,1)} %copy-done.4), channel_id=1, source_target_pairs={{0,64},{64,0},{128,192},{192,128},{256,320},{320,256},{384,448},{4... | collective-permute-start | bytes 2064392 | tf_op jit(solution)/shard_map/ppermute | solution.py:118
  85.4 1.9 %collective-permute-start.11 = (bf16[224,1536]{1,0:T(8,128)(2,1)}, bf16[224,1536]{1,0:T(8,128)(2,1)}, u32[]{:S(2)}, u32[]{:S(2)}) collective-permute-start(bf16[224,1536]{1,0:T(8,128)(2,1)} %copy-done.2), channel_id=1, source_target_pairs={{0,64},{64,0},{128,192},{192,128},{256,320},{320,256},{384,448},{4... | collective-permute-start | bytes 2064392 | tf_op jit(solution)/shard_map/ppermute | solution.py:118
  87.3 1.2 shard_map.68
  88.5 5.4 %collective-permute-start.6 = (bf16[56,1536]{1,0:T(8,128)(2,1)S(1)}, bf16[56,1536]{1,0:T(8,128)(2,1)S(1)}, u32[]{:S(2)}, u32[]{:S(2)}) collective-permute-start(bf16[56,1536]{1,0:T(8,128)(2,1)S(1)} %get-tuple-element.21), channel_id=1, source_target_pairs={{0,256},{1,257},{2,258},{3,259},{4,260},{5,261},{6,262},{7,263},{1... | collective-permute-start | bytes 516104 | tf_op jit(solution)/shard_map/ppermute | solution.py:106
  93.9 2.3 %collective-permute-start.8 = (bf16[56,1536]{1,0:T(8,128)(2,1)S(1)}, bf16[56,1536]{1,0:T(8,128)(2,1)S(1)}, u32[]{:S(2)}, u32[]{:S(2)}) collective-permute-start(bf16[56,1536]{1,0:T(8,128)(2,1)S(1)} %get-tuple-element.22), channel_id=1, source_target_pairs={{0,384},{1,385},{2,386},{3,387},{4,388},{5,389},{6,390},{7,391},{1... | collective-permute-start | bytes 516104 | tf_op jit(solution)/shard_map/ppermute | solution.py:106
  96.3 3.8 %collective-permute-start.7 = (bf16[56,1536]{1,0:T(8,128)(2,1)S(1)}, bf16[56,1536]{1,0:T(8,128)(2,1)S(1)}, u32[]{:S(2)}, u32[]{:S(2)}) collective-permute-start(bf16[56,1536]{1,0:T(8,128)(2,1)S(1)} %get-tuple-element.23), channel_id=1, source_target_pairs={{0,128},{1,129},{2,130},{3,131},{4,132},{5,133},{6,134},{7,135},{1... | collective-permute-start | bytes 516104 | tf_op jit(solution)/shard_map/ppermute | solution.py:106
  100.1 7.3 %collective-permute-start.10 = (bf16[224,768]{1,0:T(8,128)(2,1)S(1)}, bf16[224,768]{1,0:T(8,128)(2,1)S(1)}, u32[]{:S(2)}, u32[]{:S(2)}) collective-permute-start(bf16[224,768]{1,0:T(8,128)(2,1)S(1)} %get-tuple-element.15), channel_id=1, source_target_pairs={{0,64},{64,0},{128,192},{192,128},{256,320},{320,256},{384,448},{4... | collective-permute-start | bytes 1032200 | tf_op jit(solution)/shard_map/ppermute | solution.py:118
  107.5 0.7 reshape.23
  108.2 6.6 %all-to-all-start.3 = ((bf16[8,7,1536]{2,1,0:T(8,128)(2,1)}), bf16[8,7,1536]{2,1,0:T(8,128)(2,1)S(1)}, u32[]{:S(2)}, u32[]{:S(2)}) async-start(bf16[8,7,1536]{2,1,0:T(8,128)(2,1)} %reshape.23), calls=%async_computation.3 | async-start | bytes 393216 | tf_op jit(solution)/shard_map/all_to_all | solution.py:190
  114.9 3.2 %convolution_convert_fusion.1 = bf16[1536,384]{1,0:T(8,128)(2,1)} fusion(bf16[224,1536]{1,0:T(8,128)(2,1)} %collective-permute-done.9, bf16[224,1536]{1,0:T(8,128)(2,1)S(1)} %copy-done.5, bf16[224,384]{1,0:T(8,128)(2,1)S(1)} %get-tuple-element.27, bf16[224,384]{1,0:T(8,128)(2,1)S(1)} %get-tuple-element.20), kind=kOutput, calls=%fused_computation.1 | convolution fusion | flops 532512768 | bytes 2899968 | tf_op jit(solution)/shard_map/dot_general | solution.py:28
  118.1 2.9 %convolution_convert_fusion = bf16[384,1536]{1,0:T(8,128)(2,1)} fusion(bf16[224,1536]{1,0:T(8,128)(2,1)} %collective-permute-done.11, bf16[224,1536]{1,0:T(8,128)(2,1)S(1)} %copy-done.3, bf16[224,384]{1,0:T(8,128)(2,1)S(1)} %get-tuple-element.26, bf16[224,384]{1,0:T(8,128)(2,1)S(1)} %get-tuple-element.19), kind=kOutput, calls=%fused_computation | convolution fusion | flops 532512768 | bytes 2899968 | tf_op jit(solution)/shard_map/dot_general | solution.py:28
  121.1 4.4 %all-to-all-done.3 = bf16[8,7,1536]{2,1,0:T(8,128)(2,1)S(1)} async-done(((bf16[8,7,1536]{2,1,0:T(8,128)(2,1)}), bf16[8,7,1536]{2,1,0:T(8,128)(2,1)S(1)}, u32[]{:S(2)}, u32[]{:S(2)}) %all-to-all-start.3) | async-done | bytes 172064 | tf_op jit(solution)/shard_map/all_to_all | solution.py:190
  125.4 0.7 reduce_sum.22
  (35 shorter events, 0.8 us)
Async XLA Ops:
  2.2 26.4 %all-to-all-start = ((bf16[8,14,1536]{2,1,0:T(8,128)(2,1)}), bf16[8,14,1536]{2,1,0:T(8,128)(2,1)S(1)}, u32[]{:S(2)}, u32[]{:S(2)}) async-start(bf16[8,14,1536]{2,1,0:T(8,128)(2,1)} %broadcast_in_dim.4), calls=%async_computation | async-start | bytes 786432 | tf_op jit(solution)/shard_map/all_to_all | solution.py:125
  16.1 32.4 %collective-permute-start.4 = (bf16[384,1536]{1,0:T(8,128)(2,1)}, bf16[384,1536]{1,0:T(8,128)(2,1)S(1)}, u32[]{:S(2)}, u32[]{:S(2)}) collective-permute-start(bf16[384,1536]{1,0:T(8,128)(2,1)} %out0.1), channel_id=1, source_target_pairs={{0,64},{64,0},{128,192},{192,128},{256,320},{320,256},{384,448},{4... | collective-permute-start | bytes 3538952 | tf_op jit(solution)/shard_map/ppermute | solution.py:118
  18.0 30.5 %collective-permute-start.3 = (bf16[1536,384]{1,0:T(8,128)(2,1)}, bf16[1536,384]{1,0:T(8,128)(2,1)S(1)}, u32[]{:S(2)}, u32[]{:S(2)}) collective-permute-start(bf16[1536,384]{1,0:T(8,128)(2,1)} %in0.3), channel_id=1, source_target_pairs={{0,64},{64,0},{128,192},{192,128},{256,320},{320,256},{384,448},{4... | collective-permute-start | bytes 3538952 | tf_op jit(solution)/shard_map/ppermute | solution.py:118
  28.8 19.6 %copy-start = (bf16[1536,384]{1,0:T(8,128)(2,1)S(1)}, bf16[1536,384]{1,0:T(8,128)(2,1)}, u32[]{:S(2)}) copy-start(bf16[1536,384]{1,0:T(8,128)(2,1)} %in0.3) | copy-start | bytes 3538948
  28.8 19.6 %copy-start.1 = (bf16[384,1536]{1,0:T(8,128)(2,1)S(1)}, bf16[384,1536]{1,0:T(8,128)(2,1)}, u32[]{:S(2)}) copy-start(bf16[384,1536]{1,0:T(8,128)(2,1)} %out0.1) | copy-start | bytes 3538948
  28.8 9.6 %collective-permute-start.2 = (bf16[56,3072]{1,0:T(8,128)(2,1)S(1)}, bf16[56,3072]{1,0:T(8,128)(2,1)S(1)}, u32[]{:S(2)}, u32[]{:S(2)}) collective-permute-start(bf16[56,3072]{1,0:T(8,128)(2,1)S(1)} %constant_dynamic-update-slice_fusion), channel_id=1, source_target_pairs={{384,0},{385,1},{386,2},{387,3},{388,4},{389,5},{390,6},{391,7},{0... | collective-permute-start | bytes 1032200 | tf_op jit(solution)/shard_map/ppermute | solution.py:103
  31.7 11.8 %collective-permute-start.1 = (bf16[56,3072]{1,0:T(8,128)(2,1)S(1)}, bf16[56,3072]{1,0:T(8,128)(2,1)S(1)}, u32[]{:S(2)}, u32[]{:S(2)}) collective-permute-start(bf16[56,3072]{1,0:T(8,128)(2,1)S(1)} %constant_dynamic-update-slice_fusion), channel_id=1, source_target_pairs={{256,0},{257,1},{258,2},{259,3},{260,4},{261,5},{262,6},{263,7},{3... | collective-permute-start | bytes 1032200 | tf_op jit(solution)/shard_map/ppermute | solution.py:103
  34.3 14.0 %collective-permute-start = (bf16[56,3072]{1,0:T(8,128)(2,1)S(1)}, bf16[56,3072]{1,0:T(8,128)(2,1)S(1)}, u32[]{:S(2)}, u32[]{:S(2)}) collective-permute-start(bf16[56,3072]{1,0:T(8,128)(2,1)S(1)} %constant_dynamic-update-slice_fusion), channel_id=1, source_target_pairs={{128,0},{129,1},{130,2},{131,3},{132,4},{133,5},{134,6},{135,7},{2... | collective-permute-start | bytes 1032200 | tf_op jit(solution)/shard_map/ppermute | solution.py:103
  51.3 11.8 %copy-start.2 = (bf16[224,1536]{1,0:T(8,128)(2,1)}, bf16[224,1536]{1,0:T(8,128)(2,1)S(1)}, u32[]{:S(2)}) copy-start(bf16[224,1536]{1,0:T(8,128)(2,1)S(1)} %get-tuple-element.16) | copy-start | bytes 2064388
  51.3 11.8 %copy-start.4 = (bf16[224,1536]{1,0:T(8,128)(2,1)}, bf16[224,1536]{1,0:T(8,128)(2,1)S(1)}, u32[]{:S(2)}) copy-start(bf16[224,1536]{1,0:T(8,128)(2,1)S(1)} %get-tuple-element.14) | copy-start | bytes 2064388
  63.1 11.5 %collective-permute-start.5 = (bf16[56,1536]{1,0:T(8,128)(2,1)S(1)}, bf16[56,1536]{1,0:T(8,128)(2,1)S(1)}, u32[]{:S(2)}, u32[]{:S(2)}) collective-permute-start(bf16[56,1536]{1,0:T(8,128)(2,1)S(1)} %get-tuple-element.17), channel_id=1, source_target_pairs={{0,8},{8,0},{16,24},{24,16},{32,40},{40,32},{48,56},{56,48},{1,9},... | collective-permute-start | bytes 516104 | tf_op jit(solution)/shard_map/ppermute | solution.py:164
  75.7 11.6 %all-to-all-start.2 = ((bf16[4,56,1536]{2,1,0:T(8,128)(2,1)}), bf16[4,56,1536]{2,1,0:T(8,128)(2,1)S(1)}, u32[]{:S(2)}, u32[]{:S(2)}) async-start(bf16[4,56,1536]{2,1,0:T(8,128)(2,1)} %broadcast_in_dim.5), calls=%async_computation.2 | async-start | bytes 1376256 | tf_op jit(solution)/shard_map/all_to_all | solution.py:169
  79.2 35.7 %collective-permute-start.9 = (bf16[224,1536]{1,0:T(8,128)(2,1)}, bf16[224,1536]{1,0:T(8,128)(2,1)}, u32[]{:S(2)}, u32[]{:S(2)}) collective-permute-start(bf16[224,1536]{1,0:T(8,128)(2,1)} %copy-done.4), channel_id=1, source_target_pairs={{0,64},{64,0},{128,192},{192,128},{256,320},{320,256},{384,448},{4... | collective-permute-start | bytes 2064392 | tf_op jit(solution)/shard_map/ppermute | solution.py:118
  85.4 32.7 %collective-permute-start.11 = (bf16[224,1536]{1,0:T(8,128)(2,1)}, bf16[224,1536]{1,0:T(8,128)(2,1)}, u32[]{:S(2)}, u32[]{:S(2)}) collective-permute-start(bf16[224,1536]{1,0:T(8,128)(2,1)} %copy-done.2), channel_id=1, source_target_pairs={{0,64},{64,0},{128,192},{192,128},{256,320},{320,256},{384,448},{4... | collective-permute-start | bytes 2064392 | tf_op jit(solution)/shard_map/ppermute | solution.py:118
  88.5 11.6 %collective-permute-start.6 = (bf16[56,1536]{1,0:T(8,128)(2,1)S(1)}, bf16[56,1536]{1,0:T(8,128)(2,1)S(1)}, u32[]{:S(2)}, u32[]{:S(2)}) collective-permute-start(bf16[56,1536]{1,0:T(8,128)(2,1)S(1)} %get-tuple-element.21), channel_id=1, source_target_pairs={{0,256},{1,257},{2,258},{3,259},{4,260},{5,261},{6,262},{7,263},{1... | collective-permute-start | bytes 516104 | tf_op jit(solution)/shard_map/ppermute | solution.py:106
  93.9 13.5 %collective-permute-start.8 = (bf16[56,1536]{1,0:T(8,128)(2,1)S(1)}, bf16[56,1536]{1,0:T(8,128)(2,1)S(1)}, u32[]{:S(2)}, u32[]{:S(2)}) collective-permute-start(bf16[56,1536]{1,0:T(8,128)(2,1)S(1)} %get-tuple-element.22), channel_id=1, source_target_pairs={{0,384},{1,385},{2,386},{3,387},{4,388},{5,389},{6,390},{7,391},{1... | collective-permute-start | bytes 516104 | tf_op jit(solution)/shard_map/ppermute | solution.py:106
  96.3 11.1 %collective-permute-start.7 = (bf16[56,1536]{1,0:T(8,128)(2,1)S(1)}, bf16[56,1536]{1,0:T(8,128)(2,1)S(1)}, u32[]{:S(2)}, u32[]{:S(2)}) collective-permute-start(bf16[56,1536]{1,0:T(8,128)(2,1)S(1)} %get-tuple-element.23), channel_id=1, source_target_pairs={{0,128},{1,129},{2,130},{3,131},{4,132},{5,133},{6,134},{7,135},{1... | collective-permute-start | bytes 516104 | tf_op jit(solution)/shard_map/ppermute | solution.py:106
  100.1 14.8 %copy-start.5 = (bf16[224,1536]{1,0:T(8,128)(2,1)S(1)}, bf16[224,1536]{1,0:T(8,128)(2,1)}, u32[]{:S(2)}) copy-start(bf16[224,1536]{1,0:T(8,128)(2,1)} %copy-done.4) | copy-start | bytes 2064388
  100.1 14.7 %collective-permute-start.10 = (bf16[224,768]{1,0:T(8,128)(2,1)S(1)}, bf16[224,768]{1,0:T(8,128)(2,1)S(1)}, u32[]{:S(2)}, u32[]{:S(2)}) collective-permute-start(bf16[224,768]{1,0:T(8,128)(2,1)S(1)} %get-tuple-element.15), channel_id=1, source_target_pairs={{0,64},{64,0},{128,192},{192,128},{256,320},{320,256},{384,448},{4... | collective-permute-start | bytes 1032200 | tf_op jit(solution)/shard_map/ppermute | solution.py:118
  108.2 17.2 %all-to-all-start.3 = ((bf16[8,7,1536]{2,1,0:T(8,128)(2,1)}), bf16[8,7,1536]{2,1,0:T(8,128)(2,1)S(1)}, u32[]{:S(2)}, u32[]{:S(2)}) async-start(bf16[8,7,1536]{2,1,0:T(8,128)(2,1)} %reshape.23), calls=%async_computation.3 | async-start | bytes 393216 | tf_op jit(solution)/shard_map/all_to_all | solution.py:190
  114.9 3.2 %copy-start.3 = (bf16[224,1536]{1,0:T(8,128)(2,1)S(1)}, bf16[224,1536]{1,0:T(8,128)(2,1)}, u32[]{:S(2)}) copy-start(bf16[224,1536]{1,0:T(8,128)(2,1)} %copy-done.2) | copy-start | bytes 2064388

commit v5 on v4

--- a/solution.py
+++ b/solution.py
@@ -91,13 +91,14 @@
             [at(y, 1, z + d * ny) for y in range(ny) for d in range(nz // ny)] for z in range(ny)
         ]
 
-        def shift(dy, dz):
-            return [(at(y + dy, 0, z), at(y, 0, z)) for y in range(ny) for z in range(nz)] + [
-                (at(y, 1, z + dz), at(y, 1, z)) for y in range(ny) for z in range(nz)
+        def move(b):
+            step = b if b <= ny // 2 else b - ny
+            return [(at(y ^ b, 0, z), at(y, 0, z)) for y in range(ny) for z in range(nz)] + [
+                (at(y, 1, z + step), at(y, 1, z)) for y in range(ny) for z in range(nz)
             ]
 
         far = ny // 2
-        self.moves = [(b, shift(b, b if b <= far else b - ny)) for b in [far, *range(1, far), *range(far + 1, ny)]]
+        self.moves = [(b, move(b)) for b in [far, *range(ny - 1, far, -1), *range(1, far)]]
 
     def send(self, source, axes):
         return {b: lax.ppermute(source, axes, pairs) for b, pairs in self.moves}

time: 127 us -> 127 us (level)
    ppermute x5, starting transfers between devices: 19.7 us -> 21.3 us  [swap(): return lax.ppermute(v, 'gx', swap_cores)]
where the time goes in v5:
time: 127 us; the launch traced here: 126 us
  starting transfers between devices  68.3 us (54%)
  waiting for transfers between devices  30.3 us (24%)
  blocking collectives  11.6 us (9%)
  matrix products  6.12 us (5%)
  Pallas kernels  3.99 us (3%)
  local copies, waits for them, and re-layouts  2.77 us (2%)
  other arithmetic  1.92 us (2%)
    ppermute x5, starting transfers between devices, swap(): return lax.ppermute(v, 'gx', swap_cores)  21.3 us
    all_to_all x1, starting transfers between devices, per_device(): lax.all_to_all(jnp.broadcast_to(both[None], (nz, 2 * rows, width)), ('gx'...  13.9 us
    all_to_all x1, blocking collectives, per_device(): parts = lax.all_to_all(parts, 'gy', 0, 0, axis_index_groups=same_half)  11.6 us
    ppermute x3, waiting for transfers between devices, send(): return {b: lax.ppermute(source, axes, pairs) for b, pairs in self.moves}  10.9 us
    ppermute x3, starting transfers between devices, send_back(): lax.ppermute(sources[b], axes, [(d, s) for s, d in pairs])  10.8 us
    ppermute x3, starting transfers between devices, send(): return {b: lax.ppermute(source, axes, pairs) for b, pairs in self.moves}  8.55 us
    all_to_all x1, waiting for transfers between devices, per_device(): lax.all_to_all(jnp.broadcast_to(both[None], (nz, 2 * rows, width)), ('gx'...  8.16 us
    ppermute x1, waiting for transfers between devices, per_device(): sums = sums + lax.ppermute(sums.astype(bf16), 'gy', other_half).astype(f32)  6.81 us
  transfers between devices with their start and end apart: 15, of which 6 were waited for; matrix products, arithmetic and copies ran while one was open for 6% of the time, Pallas kernels for 1%

profile of v5, /device:TPU:1, one launch (start us, length us, event | category | flops | bytes accessed | tf_op | source)
XLA Modules:
  0.0 126.0 jit_solution(1957760578613217690)
XLA Ops:
  0.6 0.8 pad_maximum_fusion.2
  1.4 0.8 broadcast_in_dim.4
  2.2 13.9 %all-to-all-start = ((bf16[8,14,1536]{2,1,0:T(8,128)(2,1)}), bf16[8,14,1536]{2,1,0:T(8,128)(2,1)S(1)}, u32[]{:S(2)}, u32[]{:S(2)}) async-start(bf16[8,14,1536]{2,1,0:T(8,128)(2,1)} %broadcast_in_dim.4), calls=%async_computation | async-start | bytes 786432 | tf_op jit(solution)/shard_map/all_to_all | solution.py:126
  16.1 1.9 %collective-permute-start.4 = (bf16[384,1536]{1,0:T(8,128)(2,1)}, bf16[384,1536]{1,0:T(8,128)(2,1)S(1)}, u32[]{:S(2)}, u32[]{:S(2)}) collective-permute-start(bf16[384,1536]{1,0:T(8,128)(2,1)} %out0.1), channel_id=1, source_target_pairs={{0,64},{64,0},{128,192},{192,128},{256,320},{320,256},{384,448},{4... | collective-permute-start | bytes 3538952 | tf_op jit(solution)/shard_map/ppermute | solution.py:119
  18.0 2.4 %collective-permute-start.3 = (bf16[1536,384]{1,0:T(8,128)(2,1)}, bf16[1536,384]{1,0:T(8,128)(2,1)S(1)}, u32[]{:S(2)}, u32[]{:S(2)}) collective-permute-start(bf16[1536,384]{1,0:T(8,128)(2,1)} %in0.3), channel_id=1, source_target_pairs={{0,64},{64,0},{128,192},{192,128},{256,320},{320,256},{384,448},{4... | collective-permute-start | bytes 3538952 | tf_op jit(solution)/shard_map/ppermute | solution.py:119
  20.4 8.2 %all-to-all-done = bf16[8,14,1536]{2,1,0:T(8,128)(2,1)S(1)} async-done(((bf16[8,14,1536]{2,1,0:T(8,128)(2,1)}), bf16[8,14,1536]{2,1,0:T(8,128)(2,1)S(1)}, u32[]{:S(2)}, u32[]{:S(2)}) %all-to-all-start) | async-done | bytes 344096 | tf_op jit(solution)/shard_map/all_to_all | solution.py:126
  28.8 2.9 %collective-permute-start.2 = (bf16[56,3072]{1,0:T(8,128)(2,1)S(1)}, bf16[56,3072]{1,0:T(8,128)(2,1)S(1)}, u32[]{:S(2)}, u32[]{:S(2)}) collective-permute-start(bf16[56,3072]{1,0:T(8,128)(2,1)S(1)} %constant_dynamic-update-slice_fusion), channel_id=1, source_target_pairs={{384,0},{385,1},{386,2},{387,3},{388,4},{389,5},{390,6},{391,7},{2... | collective-permute-start | bytes 1032200 | tf_op jit(solution)/shard_map/ppermute | solution.py:104
  31.7 2.6 %collective-permute-start.1 = (bf16[56,3072]{1,0:T(8,128)(2,1)S(1)}, bf16[56,3072]{1,0:T(8,128)(2,1)S(1)}, u32[]{:S(2)}, u32[]{:S(2)}) collective-permute-start(bf16[56,3072]{1,0:T(8,128)(2,1)S(1)} %constant_dynamic-update-slice_fusion), channel_id=1, source_target_pairs={{256,0},{257,1},{258,2},{259,3},{260,4},{261,5},{262,6},{263,7},{3... | collective-permute-start | bytes 1032200 | tf_op jit(solution)/shard_map/ppermute | solution.py:104
  34.3 3.1 %collective-permute-start = (bf16[56,3072]{1,0:T(8,128)(2,1)S(1)}, bf16[56,3072]{1,0:T(8,128)(2,1)S(1)}, u32[]{:S(2)}, u32[]{:S(2)}) collective-permute-start(bf16[56,3072]{1,0:T(8,128)(2,1)S(1)} %constant_dynamic-update-slice_fusion), channel_id=1, source_target_pairs={{128,0},{129,1},{130,2},{131,3},{132,4},{133,5},{134,6},{135,7},{0... | collective-permute-start | bytes 1032200 | tf_op jit(solution)/shard_map/ppermute | solution.py:104
  37.4 1.1 collective-permute-done.2
  38.5 4.8 %collective-permute-done.1 = bf16[56,3072]{1,0:T(8,128)(2,1)S(1)} collective-permute-done((bf16[56,3072]{1,0:T(8,128)(2,1)S(1)}, bf16[56,3072]{1,0:T(8,128)(2,1)S(1)}, u32[]{:S(2)}, u32[]{:S(2)}) %collective-permute-start.1) | collective-permute-done | bytes 344096 | tf_op jit(solution)/shard_map/ppermute | solution.py:104
  43.2 5.1 %collective-permute-done = bf16[56,3072]{1,0:T(8,128)(2,1)S(1)} collective-permute-done((bf16[56,3072]{1,0:T(8,128)(2,1)S(1)}, bf16[56,3072]{1,0:T(8,128)(2,1)S(1)}, u32[]{:S(2)}, u32[]{:S(2)}) %collective-permute-start) | collective-permute-done | bytes 344096 | tf_op jit(solution)/shard_map/ppermute | solution.py:104
  48.5 2.8 %shard_map.67 = (bf16[4,56,1536]{2,1,0:T(8,128)(2,1)S(1)}, f32[56,1536]{1,0:T(8,128)S(1)}, bf16[224,1536]{1,0:T(8,128)(2,1)S(1)}, bf16[224,1536]{1,0:T(8,128)(2,1)S(1)}) custom-call(bf16[224,3072]{1,0:T(8,128)(2,1)S(1)} %pad_maximum_fusion.own_ref, bf16[1536,384]{1,0:T(8,128)(2,1)S(1)} %copy-done, bf16[1536,384]{1,0:T(8,128)(2,1)S(1)} %collective-permute-done.3.in1, ...), custom_call_target="tpu_custom_call" | custom-call | flops 1056964608 | bytes 4718592 | tf_op jit(solution)/shard_map/pallas_call | solution.py:141
  51.3 11.6 %all_to_all.20 = bf16[4,56,1536]{2,1,0:T(8,128)(2,1)S(1)} all-to-all(bf16[4,56,1536]{2,1,0:T(8,128)(2,1)S(1)} %get-tuple-element.11), channel_id=1, replica_groups={{0,16,32,48},{8,24,40,56},{1,17,33,49},{9,25,41,57},{2,18,34,50},{10,26..., dimensions={0} | all-to-all | bytes 1376256 | tf_op jit(solution)/shard_map/all_to_all | solution.py:163
  63.1 4.4 %collective-permute-start.5 = (bf16[56,1536]{1,0:T(8,128)(2,1)S(1)}, bf16[56,1536]{1,0:T(8,128)(2,1)S(1)}, u32[]{:S(2)}, u32[]{:S(2)}) collective-permute-start(bf16[56,1536]{1,0:T(8,128)(2,1)S(1)} %get-tuple-element.17), channel_id=1, source_target_pairs={{0,8},{8,0},{16,24},{24,16},{32,40},{40,32},{48,56},{56,48},{1,9},... | collective-permute-start | bytes 516104 | tf_op jit(solution)/shard_map/ppermute | solution.py:165
  67.5 6.8 %collective-permute-done.5 = bf16[56,1536]{1,0:T(8,128)(2,1)S(1)} collective-permute-done((bf16[56,1536]{1,0:T(8,128)(2,1)S(1)}, bf16[56,1536]{1,0:T(8,128)(2,1)S(1)}, u32[]{:S(2)}, u32[]{:S(2)}) %collective-permute-start.5) | collective-permute-done | bytes 172064 | tf_op jit(solution)/shard_map/ppermute | solution.py:165
  74.4 0.1 multiply_convert_fusion
  74.5 0.9 broadcast_in_dim.5
  75.4 3.5 %all-to-all-start.2 = ((bf16[4,56,1536]{2,1,0:T(8,128)(2,1)}), bf16[4,56,1536]{2,1,0:T(8,128)(2,1)S(1)}, u32[]{:S(2)}, u32[]{:S(2)}) async-start(bf16[4,56,1536]{2,1,0:T(8,128)(2,1)} %broadcast_in_dim.5), calls=%async_computation.2 | async-start | bytes 1376256 | tf_op jit(solution)/shard_map/all_to_all | solution.py:170
  78.9 8.6 %collective-permute-start.9 = (bf16[224,1536]{1,0:T(8,128)(2,1)}, bf16[224,1536]{1,0:T(8,128)(2,1)}, u32[]{:S(2)}, u32[]{:S(2)}) collective-permute-start(bf16[224,1536]{1,0:T(8,128)(2,1)} %copy-done.4), channel_id=1, source_target_pairs={{0,64},{64,0},{128,192},{192,128},{256,320},{320,256},{384,448},{4... | collective-permute-start | bytes 2064392 | tf_op jit(solution)/shard_map/ppermute | solution.py:119
  87.5 1.9 %collective-permute-start.11 = (bf16[224,1536]{1,0:T(8,128)(2,1)}, bf16[224,1536]{1,0:T(8,128)(2,1)}, u32[]{:S(2)}, u32[]{:S(2)}) collective-permute-start(bf16[224,1536]{1,0:T(8,128)(2,1)} %copy-done.2), channel_id=1, source_target_pairs={{0,64},{64,0},{128,192},{192,128},{256,320},{320,256},{384,448},{4... | collective-permute-start | bytes 2064392 | tf_op jit(solution)/shard_map/ppermute | solution.py:119
  89.5 1.2 shard_map.68
  90.7 4.3 %collective-permute-start.6 = (bf16[56,1536]{1,0:T(8,128)(2,1)S(1)}, bf16[56,1536]{1,0:T(8,128)(2,1)S(1)}, u32[]{:S(2)}, u32[]{:S(2)}) collective-permute-start(bf16[56,1536]{1,0:T(8,128)(2,1)S(1)} %get-tuple-element.21), channel_id=1, source_target_pairs={{0,256},{1,257},{2,258},{3,259},{4,260},{5,261},{6,262},{7,263},{1... | collective-permute-start | bytes 516104 | tf_op jit(solution)/shard_map/ppermute | solution.py:107
  95.0 3.7 %collective-permute-start.8 = (bf16[56,1536]{1,0:T(8,128)(2,1)S(1)}, bf16[56,1536]{1,0:T(8,128)(2,1)S(1)}, u32[]{:S(2)}, u32[]{:S(2)}) collective-permute-start(bf16[56,1536]{1,0:T(8,128)(2,1)S(1)} %get-tuple-element.22), channel_id=1, source_target_pairs={{0,128},{1,129},{2,130},{3,131},{4,132},{5,133},{6,134},{7,135},{1... | collective-permute-start | bytes 516104 | tf_op jit(solution)/shard_map/ppermute | solution.py:107
  98.7 2.8 %collective-permute-start.7 = (bf16[56,1536]{1,0:T(8,128)(2,1)S(1)}, bf16[56,1536]{1,0:T(8,128)(2,1)S(1)}, u32[]{:S(2)}, u32[]{:S(2)}) collective-permute-start(bf16[56,1536]{1,0:T(8,128)(2,1)S(1)} %get-tuple-element.23), channel_id=1, source_target_pairs={{0,384},{1,385},{2,386},{3,387},{4,388},{5,389},{6,390},{7,391},{1... | collective-permute-start | bytes 516104 | tf_op jit(solution)/shard_map/ppermute | solution.py:107
  101.6 6.4 %collective-permute-start.10 = (bf16[224,768]{1,0:T(8,128)(2,1)S(1)}, bf16[224,768]{1,0:T(8,128)(2,1)S(1)}, u32[]{:S(2)}, u32[]{:S(2)}) collective-permute-start(bf16[224,768]{1,0:T(8,128)(2,1)S(1)} %get-tuple-element.15), channel_id=1, source_target_pairs={{0,64},{64,0},{128,192},{192,128},{256,320},{320,256},{384,448},{4... | collective-permute-start | bytes 1032200 | tf_op jit(solution)/shard_map/ppermute | solution.py:119
  108.1 0.7 reshape.23
  108.9 5.9 %all-to-all-start.3 = ((bf16[8,7,1536]{2,1,0:T(8,128)(2,1)}), bf16[8,7,1536]{2,1,0:T(8,128)(2,1)S(1)}, u32[]{:S(2)}, u32[]{:S(2)}) async-start(bf16[8,7,1536]{2,1,0:T(8,128)(2,1)} %reshape.23), calls=%async_computation.3 | async-start | bytes 393216 | tf_op jit(solution)/shard_map/all_to_all | solution.py:191
  114.8 3.2 %convolution_convert_fusion.1 = bf16[1536,384]{1,0:T(8,128)(2,1)} fusion(bf16[224,1536]{1,0:T(8,128)(2,1)} %collective-permute-done.9, bf16[224,1536]{1,0:T(8,128)(2,1)S(1)} %copy-done.5, bf16[224,384]{1,0:T(8,128)(2,1)S(1)} %get-tuple-element.27, bf16[224,384]{1,0:T(8,128)(2,1)S(1)} %get-tuple-element.20), kind=kOutput, calls=%fused_computation.1 | convolution fusion | flops 532512768 | bytes 2899968 | tf_op jit(solution)/shard_map/dot_general | solution.py:28
  118.0 2.9 %convolution_convert_fusion = bf16[384,1536]{1,0:T(8,128)(2,1)} fusion(bf16[224,1536]{1,0:T(8,128)(2,1)} %collective-permute-done.11, bf16[224,1536]{1,0:T(8,128)(2,1)S(1)} %copy-done.3, bf16[224,384]{1,0:T(8,128)(2,1)S(1)} %get-tuple-element.26, bf16[224,384]{1,0:T(8,128)(2,1)S(1)} %get-tuple-element.19), kind=kOutput, calls=%fused_computation | convolution fusion | flops 532512768 | bytes 2899968 | tf_op jit(solution)/shard_map/dot_general | solution.py:28
  121.0 4.4 %all-to-all-done.3 = bf16[8,7,1536]{2,1,0:T(8,128)(2,1)S(1)} async-done(((bf16[8,7,1536]{2,1,0:T(8,128)(2,1)}), bf16[8,7,1536]{2,1,0:T(8,128)(2,1)S(1)}, u32[]{:S(2)}, u32[]{:S(2)}) %all-to-all-start.3) | async-done | bytes 172064 | tf_op jit(solution)/shard_map/all_to_all | solution.py:191
  125.3 0.7 reduce_sum.22
  (35 shorter events, 0.8 us)
Async XLA Ops:
  2.2 26.4 %all-to-all-start = ((bf16[8,14,1536]{2,1,0:T(8,128)(2,1)}), bf16[8,14,1536]{2,1,0:T(8,128)(2,1)S(1)}, u32[]{:S(2)}, u32[]{:S(2)}) async-start(bf16[8,14,1536]{2,1,0:T(8,128)(2,1)} %broadcast_in_dim.4), calls=%async_computation | async-start | bytes 786432 | tf_op jit(solution)/shard_map/all_to_all | solution.py:126
  16.1 32.4 %collective-permute-start.4 = (bf16[384,1536]{1,0:T(8,128)(2,1)}, bf16[384,1536]{1,0:T(8,128)(2,1)S(1)}, u32[]{:S(2)}, u32[]{:S(2)}) collective-permute-start(bf16[384,1536]{1,0:T(8,128)(2,1)} %out0.1), channel_id=1, source_target_pairs={{0,64},{64,0},{128,192},{192,128},{256,320},{320,256},{384,448},{4... | collective-permute-start | bytes 3538952 | tf_op jit(solution)/shard_map/ppermute | solution.py:119
  18.0 30.5 %collective-permute-start.3 = (bf16[1536,384]{1,0:T(8,128)(2,1)}, bf16[1536,384]{1,0:T(8,128)(2,1)S(1)}, u32[]{:S(2)}, u32[]{:S(2)}) collective-permute-start(bf16[1536,384]{1,0:T(8,128)(2,1)} %in0.3), channel_id=1, source_target_pairs={{0,64},{64,0},{128,192},{192,128},{256,320},{320,256},{384,448},{4... | collective-permute-start | bytes 3538952 | tf_op jit(solution)/shard_map/ppermute | solution.py:119
  28.8 19.6 %copy-start = (bf16[1536,384]{1,0:T(8,128)(2,1)S(1)}, bf16[1536,384]{1,0:T(8,128)(2,1)}, u32[]{:S(2)}) copy-start(bf16[1536,384]{1,0:T(8,128)(2,1)} %in0.3) | copy-start | bytes 3538948
  28.8 19.6 %copy-start.1 = (bf16[384,1536]{1,0:T(8,128)(2,1)S(1)}, bf16[384,1536]{1,0:T(8,128)(2,1)}, u32[]{:S(2)}) copy-start(bf16[384,1536]{1,0:T(8,128)(2,1)} %out0.1) | copy-start | bytes 3538948
  28.8 9.6 %collective-permute-start.2 = (bf16[56,3072]{1,0:T(8,128)(2,1)S(1)}, bf16[56,3072]{1,0:T(8,128)(2,1)S(1)}, u32[]{:S(2)}, u32[]{:S(2)}) collective-permute-start(bf16[56,3072]{1,0:T(8,128)(2,1)S(1)} %constant_dynamic-update-slice_fusion), channel_id=1, source_target_pairs={{384,0},{385,1},{386,2},{387,3},{388,4},{389,5},{390,6},{391,7},{2... | collective-permute-start | bytes 1032200 | tf_op jit(solution)/shard_map/ppermute | solution.py:104
  31.7 11.5 %collective-permute-start.1 = (bf16[56,3072]{1,0:T(8,128)(2,1)S(1)}, bf16[56,3072]{1,0:T(8,128)(2,1)S(1)}, u32[]{:S(2)}, u32[]{:S(2)}) collective-permute-start(bf16[56,3072]{1,0:T(8,128)(2,1)S(1)} %constant_dynamic-update-slice_fusion), channel_id=1, source_target_pairs={{256,0},{257,1},{258,2},{259,3},{260,4},{261,5},{262,6},{263,7},{3... | collective-permute-start | bytes 1032200 | tf_op jit(solution)/shard_map/ppermute | solution.py:104
  34.3 14.0 %collective-permute-start = (bf16[56,3072]{1,0:T(8,128)(2,1)S(1)}, bf16[56,3072]{1,0:T(8,128)(2,1)S(1)}, u32[]{:S(2)}, u32[]{:S(2)}) collective-permute-start(bf16[56,3072]{1,0:T(8,128)(2,1)S(1)} %constant_dynamic-update-slice_fusion), channel_id=1, source_target_pairs={{128,0},{129,1},{130,2},{131,3},{132,4},{133,5},{134,6},{135,7},{0... | collective-permute-start | bytes 1032200 | tf_op jit(solution)/shard_map/ppermute | solution.py:104
  51.3 11.8 %copy-start.2 = (bf16[224,1536]{1,0:T(8,128)(2,1)}, bf16[224,1536]{1,0:T(8,128)(2,1)S(1)}, u32[]{:S(2)}) copy-start(bf16[224,1536]{1,0:T(8,128)(2,1)S(1)} %get-tuple-element.16) | copy-start | bytes 2064388
  51.3 11.8 %copy-start.4 = (bf16[224,1536]{1,0:T(8,128)(2,1)}, bf16[224,1536]{1,0:T(8,128)(2,1)S(1)}, u32[]{:S(2)}) copy-start(bf16[224,1536]{1,0:T(8,128)(2,1)S(1)} %get-tuple-element.14) | copy-start | bytes 2064388
  63.1 11.2 %collective-permute-start.5 = (bf16[56,1536]{1,0:T(8,128)(2,1)S(1)}, bf16[56,1536]{1,0:T(8,128)(2,1)S(1)}, u32[]{:S(2)}, u32[]{:S(2)}) collective-permute-start(bf16[56,1536]{1,0:T(8,128)(2,1)S(1)} %get-tuple-element.17), channel_id=1, source_target_pairs={{0,8},{8,0},{16,24},{24,16},{32,40},{40,32},{48,56},{56,48},{1,9},... | collective-permute-start | bytes 516104 | tf_op jit(solution)/shard_map/ppermute | solution.py:165
  75.4 14.1 %all-to-all-start.2 = ((bf16[4,56,1536]{2,1,0:T(8,128)(2,1)}), bf16[4,56,1536]{2,1,0:T(8,128)(2,1)S(1)}, u32[]{:S(2)}, u32[]{:S(2)}) async-start(bf16[4,56,1536]{2,1,0:T(8,128)(2,1)} %broadcast_in_dim.5), calls=%async_computation.2 | async-start | bytes 1376256 | tf_op jit(solution)/shard_map/all_to_all | solution.py:170
  78.9 35.9 %collective-permute-start.9 = (bf16[224,1536]{1,0:T(8,128)(2,1)}, bf16[224,1536]{1,0:T(8,128)(2,1)}, u32[]{:S(2)}, u32[]{:S(2)}) collective-permute-start(bf16[224,1536]{1,0:T(8,128)(2,1)} %copy-done.4), channel_id=1, source_target_pairs={{0,64},{64,0},{128,192},{192,128},{256,320},{320,256},{384,448},{4... | collective-permute-start | bytes 2064392 | tf_op jit(solution)/shard_map/ppermute | solution.py:119
  87.5 30.5 %collective-permute-start.11 = (bf16[224,1536]{1,0:T(8,128)(2,1)}, bf16[224,1536]{1,0:T(8,128)(2,1)}, u32[]{:S(2)}, u32[]{:S(2)}) collective-permute-start(bf16[224,1536]{1,0:T(8,128)(2,1)} %copy-done.2), channel_id=1, source_target_pairs={{0,64},{64,0},{128,192},{192,128},{256,320},{320,256},{384,448},{4... | collective-permute-start | bytes 2064392 | tf_op jit(solution)/shard_map/ppermute | solution.py:119
  90.7 10.9 %collective-permute-start.6 = (bf16[56,1536]{1,0:T(8,128)(2,1)S(1)}, bf16[56,1536]{1,0:T(8,128)(2,1)S(1)}, u32[]{:S(2)}, u32[]{:S(2)}) collective-permute-start(bf16[56,1536]{1,0:T(8,128)(2,1)S(1)} %get-tuple-element.21), channel_id=1, source_target_pairs={{0,256},{1,257},{2,258},{3,259},{4,260},{5,261},{6,262},{7,263},{1... | collective-permute-start | bytes 516104 | tf_op jit(solution)/shard_map/ppermute | solution.py:107
  95.0 13.0 %collective-permute-start.8 = (bf16[56,1536]{1,0:T(8,128)(2,1)S(1)}, bf16[56,1536]{1,0:T(8,128)(2,1)S(1)}, u32[]{:S(2)}, u32[]{:S(2)}) collective-permute-start(bf16[56,1536]{1,0:T(8,128)(2,1)S(1)} %get-tuple-element.22), channel_id=1, source_target_pairs={{0,128},{1,129},{2,130},{3,131},{4,132},{5,133},{6,134},{7,135},{1... | collective-permute-start | bytes 516104 | tf_op jit(solution)/shard_map/ppermute | solution.py:107
  98.7 9.3 %collective-permute-start.7 = (bf16[56,1536]{1,0:T(8,128)(2,1)S(1)}, bf16[56,1536]{1,0:T(8,128)(2,1)S(1)}, u32[]{:S(2)}, u32[]{:S(2)}) collective-permute-start(bf16[56,1536]{1,0:T(8,128)(2,1)S(1)} %get-tuple-element.23), channel_id=1, source_target_pairs={{0,384},{1,385},{2,386},{3,387},{4,388},{5,389},{6,390},{7,391},{1... | collective-permute-start | bytes 516104 | tf_op jit(solution)/shard_map/ppermute | solution.py:107
  101.6 13.2 %copy-start.5 = (bf16[224,1536]{1,0:T(8,128)(2,1)S(1)}, bf16[224,1536]{1,0:T(8,128)(2,1)}, u32[]{:S(2)}) copy-start(bf16[224,1536]{1,0:T(8,128)(2,1)} %copy-done.4) | copy-start | bytes 2064388
  101.6 13.1 %collective-permute-start.10 = (bf16[224,768]{1,0:T(8,128)(2,1)S(1)}, bf16[224,768]{1,0:T(8,128)(2,1)S(1)}, u32[]{:S(2)}, u32[]{:S(2)}) collective-permute-start(bf16[224,768]{1,0:T(8,128)(2,1)S(1)} %get-tuple-element.15), channel_id=1, source_target_pairs={{0,64},{64,0},{128,192},{192,128},{256,320},{320,256},{384,448},{4... | collective-permute-start | bytes 1032200 | tf_op jit(solution)/shard_map/ppermute | solution.py:119
  108.9 16.5 %all-to-all-start.3 = ((bf16[8,7,1536]{2,1,0:T(8,128)(2,1)}), bf16[8,7,1536]{2,1,0:T(8,128)(2,1)S(1)}, u32[]{:S(2)}, u32[]{:S(2)}) async-start(bf16[8,7,1536]{2,1,0:T(8,128)(2,1)} %reshape.23), calls=%async_computation.3 | async-start | bytes 393216 | tf_op jit(solution)/shard_map/all_to_all | solution.py:191
  114.8 3.2 %copy-start.3 = (bf16[224,1536]{1,0:T(8,128)(2,1)S(1)}, bf16[224,1536]{1,0:T(8,128)(2,1)}, u32[]{:S(2)}) copy-start(bf16[224,1536]{1,0:T(8,128)(2,1)} %copy-done.2) | copy-start | bytes 2064388

commit v6 on v5

--- a/solution.py
+++ b/solution.py
@@ -29,7 +29,7 @@
 
 
 def first_products(
-    own_ref, in0, in1, out0, out1, parts_ref, mine_ref, kept_in, kept_grad, held_in, held_out, total, sems
+    own_ref, in0, in1, out0, out1, parts_ref, mine_ref, kept_ref, held_in, held_out, total, sems
 ):
     width, hidden = in0.shape
     blocks, share, _ = parts_ref.shape
@@ -38,8 +38,8 @@
         pltpu.make_async_copy(in1, held_in.at[:, hidden:], sems.at[1]),
         pltpu.make_async_copy(out0, held_out.at[:hidden], sems.at[2]),
         pltpu.make_async_copy(out1, held_out.at[hidden:], sems.at[3]),
-        pltpu.make_async_copy(own_ref.at[:, :width], kept_in, sems.at[4]),
-        pltpu.make_async_copy(own_ref.at[:, width:], kept_grad, sems.at[5]),
+        pltpu.make_async_copy(own_ref.at[:, :width], kept_ref.at[0], sems.at[4]),
+        pltpu.make_async_copy(own_ref.at[:, width:], kept_ref.at[1], sems.at[5]),
     ]
     for copy in copies:
         copy.start()
@@ -138,16 +138,15 @@
 
     vmem, anywhere = pl.BlockSpec(memory_space=pltpu.VMEM), pl.BlockSpec(memory_space=pl.ANY)
     mib = 1024 * 1024
-    parts, mine, kept_in, kept_grad = pl.pallas_call(
+    parts, mine, kept = pl.pallas_call(
         first_products,
         out_shape=(
             jax.ShapeDtypeStruct((blocks, share, 4 * hidden), bf16),
             jax.ShapeDtypeStruct((share, 4 * hidden), f32),
-            jax.ShapeDtypeStruct((tokens, width), bf16),
-            jax.ShapeDtypeStruct((tokens, width), bf16),
+            jax.ShapeDtypeStruct((2, tokens, width), bf16),
         ),
         in_specs=[vmem] + [anywhere] * 4,
-        out_specs=(vmem, vmem, anywhere, anywhere),
+        out_specs=(vmem, vmem, anywhere),
         scratch_shapes=[
             pltpu.VMEM((width, 2 * hidden), bf16),
             pltpu.VMEM((2 * hidden, width), bf16),
@@ -159,7 +158,7 @@
             flops=8 * tokens * width * hidden, bytes_accessed=8 * width * hidden, transcendentals=0
         ),
     )(own, weight_in, other_in, weight_out, other_out)
-    swapped_in, swapped_grad = swap(kept_in), swap(kept_grad)
+    swapped = swap(kept)
     parts = lax.all_to_all(parts, "gy", 0, 0, axis_index_groups=same_half)
     sums = mine + jnp.sum(parts.astype(f32), axis=0)
     sums = sums + lax.ppermute(sums.astype(bf16), "gy", other_half).astype(f32)
@@ -194,10 +193,10 @@
     grad_inputs = jnp.sum(pieces.astype(f32), axis=0).astype(bf16)
     grad_weight_out = contract_first(
         jnp.concatenate([whole[:, :hidden], swapped_whole[:, :hidden]], axis=0),
-        jnp.concatenate([kept_grad, swapped_grad], axis=0),
+        jnp.concatenate([kept[1], swapped[1]], axis=0),
     ).astype(bf16)
     grad_weight_in = contract_first(
-        jnp.concatenate([kept_in, swapped_in], axis=0),
+        jnp.concatenate([kept[0], swapped[0]], axis=0),
         jnp.concatenate([whole[:, 2 * hidden : 3 * hidden], swapped_whole[:, hidden:]], axis=0),
     ).astype(bf16)
     return (grad_inputs, grad_weight_in, grad_weight_out)

time: 127 us -> 129 us (1.016)
  local copies, waits for them, and re-layouts: 2.77 us -> 8.44 us
  starting transfers between devices: 68.3 us -> 66 us
  matrix products: 6.12 us -> 3.86 us
  waiting for transfers between devices: 30.3 us -> 31.6 us
    ppermute x1, waiting for transfers between devices: 6.81 us -> 0.01 us  [per_device(): sums = sums + lax.ppermute(sums.astype(bf16), 'gy', other_half).astype(f32)]
    all_to_all x1, waiting for transfers between devices: 0.01 us -> 5.29 us  [per_device(): lax.all_to_all(jnp.broadcast_to(done[None], (blocks, share, 4 * hidden)),...]
    squeeze x0 -> x2, local copies, waits for them, and re-layouts: none -> 3.95 us  [the longest x1 2.48 us: per_device(): kept[1]]
    ppermute x3, waiting for transfers between devices: 0.01 us -> 2.84 us  [send_back(): lax.ppermute(sources[b], axes, [(d, s) for s, d in pairs])]
    dot_general x2, matrix products: 6.12 us -> 3.86 us  [contract_first(): lax.dot_general(left, right, (((0,), (0,)), ((), ())), preferred_element_...]
    all_to_all x1, starting transfers between devices: 5.88 us -> 3.95 us  [per_device(): lax.all_to_all(total.astype(bf16).reshape(nz, rows, width), ('gx', 'gz'),...]
    ppermute x5 -> x4, starting transfers between devices: 21.3 us -> 20.9 us  [swap(): return lax.ppermute(v, 'gx', swap_cores)]
  transfers between devices with their start and end apart: 15 -> 14, of which waited for: 6 -> 8; matrix products, arithmetic and copies ran while one was open for 6% -> 9% of each run, Pallas kernels for 1% -> 1%
where the time goes in v6:
time: 129 us; the launch traced here: 128 us
  starting transfers between devices  66 us (51%)
  waiting for transfers between devices  31.6 us (24%)
  blocking collectives  11.6 us (9%)
  local copies, waits for them, and re-layouts  8.44 us (7%)
  Pallas kernels  3.89 us (3%)
  matrix products  3.86 us (3%)
  other arithmetic  1.92 us (1%)
    ppermute x4, starting transfers between devices, swap(): return lax.ppermute(v, 'gx', swap_cores)  20.9 us
    all_to_all x1, starting transfers between devices, per_device(): lax.all_to_all(jnp.broadcast_to(both[None], (nz, 2 * rows, width)), ('gx'...  13.9 us
    all_to_all x1, blocking collectives, per_device(): parts = lax.all_to_all(parts, 'gy', 0, 0, axis_index_groups=same_half)  11.6 us
    ppermute x3, waiting for transfers between devices, send(): return {b: lax.ppermute(source, axes, pairs) for b, pairs in self.moves}  10.9 us
    ppermute x3, starting transfers between devices, send_back(): lax.ppermute(sources[b], axes, [(d, s) for s, d in pairs])  10.8 us
    ppermute x3, starting transfers between devices, send(): return {b: lax.ppermute(source, axes, pairs) for b, pairs in self.moves}  8.55 us
    all_to_all x1, waiting for transfers between devices, per_device(): lax.all_to_all(jnp.broadcast_to(both[None], (nz, 2 * rows, width)), ('gx'...  8.16 us
    all_to_all x1, waiting for transfers between devices, per_device(): lax.all_to_all(jnp.broadcast_to(done[None], (blocks, share, 4 * hidden)),...  5.29 us
  transfers between devices with their start and end apart: 14, of which 8 were waited for; matrix products, arithmetic and copies ran while one was open for 9% of the time, Pallas kernels for 1%

profile of v6, /device:TPU:1, one launch (start us, length us, event | category | flops | bytes accessed | tf_op | source)
XLA Modules:
  0.0 128.2 jit_solution(13625644927357896218)
XLA Ops:
  0.6 0.8 pad_maximum_fusion.2
  1.4 0.8 broadcast_in_dim.4
  2.2 13.9 %all-to-all-start = ((bf16[8,14,1536]{2,1,0:T(8,128)(2,1)}), bf16[8,14,1536]{2,1,0:T(8,128)(2,1)S(1)}, u32[]{:S(2)}, u32[]{:S(2)}) async-start(bf16[8,14,1536]{2,1,0:T(8,128)(2,1)} %broadcast_in_dim.4), calls=%async_computation | async-start | bytes 786432 | tf_op jit(solution)/shard_map/all_to_all | solution.py:126
  16.1 1.9 %collective-permute-start.4 = (bf16[384,1536]{1,0:T(8,128)(2,1)}, bf16[384,1536]{1,0:T(8,128)(2,1)S(1)}, u32[]{:S(2)}, u32[]{:S(2)}) collective-permute-start(bf16[384,1536]{1,0:T(8,128)(2,1)} %out0.1), channel_id=1, source_target_pairs={{0,64},{64,0},{128,192},{192,128},{256,320},{320,256},{384,448},{4... | collective-permute-start | bytes 3538952 | tf_op jit(solution)/shard_map/ppermute | solution.py:119
  18.0 2.4 %collective-permute-start.3 = (bf16[1536,384]{1,0:T(8,128)(2,1)}, bf16[1536,384]{1,0:T(8,128)(2,1)S(1)}, u32[]{:S(2)}, u32[]{:S(2)}) collective-permute-start(bf16[1536,384]{1,0:T(8,128)(2,1)} %in0.3), channel_id=1, source_target_pairs={{0,64},{64,0},{128,192},{192,128},{256,320},{320,256},{384,448},{4... | collective-permute-start | bytes 3538952 | tf_op jit(solution)/shard_map/ppermute | solution.py:119
  20.4 8.2 %all-to-all-done = bf16[8,14,1536]{2,1,0:T(8,128)(2,1)S(1)} async-done(((bf16[8,14,1536]{2,1,0:T(8,128)(2,1)}), bf16[8,14,1536]{2,1,0:T(8,128)(2,1)S(1)}, u32[]{:S(2)}, u32[]{:S(2)}) %all-to-all-start) | async-done | bytes 344096 | tf_op jit(solution)/shard_map/all_to_all | solution.py:126
  28.8 2.9 %collective-permute-start.2 = (bf16[56,3072]{1,0:T(8,128)(2,1)S(1)}, bf16[56,3072]{1,0:T(8,128)(2,1)S(1)}, u32[]{:S(2)}, u32[]{:S(2)}) collective-permute-start(bf16[56,3072]{1,0:T(8,128)(2,1)S(1)} %constant_dynamic-update-slice_fusion), channel_id=1, source_target_pairs={{384,0},{385,1},{386,2},{387,3},{388,4},{389,5},{390,6},{391,7},{2... | collective-permute-start | bytes 1032200 | tf_op jit(solution)/shard_map/ppermute | solution.py:104
  31.7 2.6 %collective-permute-start.1 = (bf16[56,3072]{1,0:T(8,128)(2,1)S(1)}, bf16[56,3072]{1,0:T(8,128)(2,1)S(1)}, u32[]{:S(2)}, u32[]{:S(2)}) collective-permute-start(bf16[56,3072]{1,0:T(8,128)(2,1)S(1)} %constant_dynamic-update-slice_fusion), channel_id=1, source_target_pairs={{256,0},{257,1},{258,2},{259,3},{260,4},{261,5},{262,6},{263,7},{3... | collective-permute-start | bytes 1032200 | tf_op jit(solution)/shard_map/ppermute | solution.py:104
  34.3 3.1 %collective-permute-start = (bf16[56,3072]{1,0:T(8,128)(2,1)S(1)}, bf16[56,3072]{1,0:T(8,128)(2,1)S(1)}, u32[]{:S(2)}, u32[]{:S(2)}) collective-permute-start(bf16[56,3072]{1,0:T(8,128)(2,1)S(1)} %constant_dynamic-update-slice_fusion), channel_id=1, source_target_pairs={{128,0},{129,1},{130,2},{131,3},{132,4},{133,5},{134,6},{135,7},{0... | collective-permute-start | bytes 1032200 | tf_op jit(solution)/shard_map/ppermute | solution.py:104
  37.4 1.1 collective-permute-done.2
  38.5 4.8 %collective-permute-done.1 = bf16[56,3072]{1,0:T(8,128)(2,1)S(1)} collective-permute-done((bf16[56,3072]{1,0:T(8,128)(2,1)S(1)}, bf16[56,3072]{1,0:T(8,128)(2,1)S(1)}, u32[]{:S(2)}, u32[]{:S(2)}) %collective-permute-start.1) | collective-permute-done | bytes 344096 | tf_op jit(solution)/shard_map/ppermute | solution.py:104
  43.2 5.1 %collective-permute-done = bf16[56,3072]{1,0:T(8,128)(2,1)S(1)} collective-permute-done((bf16[56,3072]{1,0:T(8,128)(2,1)S(1)}, bf16[56,3072]{1,0:T(8,128)(2,1)S(1)}, u32[]{:S(2)}, u32[]{:S(2)}) %collective-permute-start) | collective-permute-done | bytes 344096 | tf_op jit(solution)/shard_map/ppermute | solution.py:104
  48.5 2.7 %shard_map.67 = (bf16[4,56,1536]{2,1,0:T(8,128)(2,1)S(1)}, f32[56,1536]{1,0:T(8,128)S(1)}, bf16[2,224,1536]{2,1,0:T(8,128)(2,1)}) custom-call(bf16[224,3072]{1,0:T(8,128)(2,1)S(1)} %pad_maximum_fusion.own_ref, bf16[1536,384]{1,0:T(8,128)(2,1)S(1)} %copy-done, bf16[1536,384]{1,0:T(8,128)(2,1)S(1)} %collective-permute-done.3.in1, ...), custom_call_target="tpu_custom_call" | custom-call | flops 1056964608 | bytes 4718592 | tf_op jit(solution)/shard_map/pallas_call | solution.py:141
  51.2 11.6 %all_to_all.20 = bf16[4,56,1536]{2,1,0:T(8,128)(2,1)S(1)} all-to-all(bf16[4,56,1536]{2,1,0:T(8,128)(2,1)S(1)} %get-tuple-element.10), channel_id=1, replica_groups={{0,16,32,48},{8,24,40,56},{1,17,33,49},{9,25,41,57},{2,18,34,50},{10,26..., dimensions={0} | all-to-all | bytes 1376256 | tf_op jit(solution)/shard_map/all_to_all | solution.py:162
  63.0 4.4 %collective-permute-start.5 = (bf16[56,1536]{1,0:T(8,128)(2,1)S(1)}, bf16[56,1536]{1,0:T(8,128)(2,1)S(1)}, u32[]{:S(2)}, u32[]{:S(2)}) collective-permute-start(bf16[56,1536]{1,0:T(8,128)(2,1)S(1)} %get-tuple-element.15), channel_id=1, source_target_pairs={{0,8},{8,0},{16,24},{24,16},{32,40},{40,32},{48,56},{56,48},{1,9},... | collective-permute-start | bytes 516104 | tf_op jit(solution)/shard_map/ppermute | solution.py:164
  67.4 8.9 %collective-permute-start.9 = (bf16[2,224,1536]{2,1,0:T(8,128)(2,1)}, bf16[2,224,1536]{2,1,0:T(8,128)(2,1)}, u32[]{:S(2)}, u32[]{:S(2)}) collective-permute-start(bf16[2,224,1536]{2,1,0:T(8,128)(2,1)} %get-tuple-element.13), channel_id=1, source_target_pairs={{0,64},{64,0},{128,192},{192,128},{256,320},{320,256},{384,448},{4... | collective-permute-start | bytes 4128776 | tf_op jit(solution)/shard_map/ppermute | solution.py:119
  76.5 0.9 broadcast_in_dim.5
  77.4 3.5 %all-to-all-start.2 = ((bf16[4,56,1536]{2,1,0:T(8,128)(2,1)}), bf16[4,56,1536]{2,1,0:T(8,128)(2,1)S(1)}, u32[]{:S(2)}, u32[]{:S(2)}) async-start(bf16[4,56,1536]{2,1,0:T(8,128)(2,1)} %broadcast_in_dim.5), calls=%async_computation.2 | async-start | bytes 1376256 | tf_op jit(solution)/shard_map/all_to_all | solution.py:169
  80.9 2.5 %slice_bitcast_fusion.2 = (bf16[224,1536]{1,0:T(8,128)(2,1)}, bf16[224,1536]{1,0:T(8,128)(2,1)}) fusion(bf16[2,224,1536]{2,1,0:T(8,128)(2,1)} %get-tuple-element.13), kind=kLoop, calls=%fused_computation.12 | loop fusion | bytes 2752512 | tf_op jit(solution)/shard_map/squeeze | solution.py:196
  83.3 5.3 %all-to-all-done.2 = bf16[4,56,1536]{2,1,0:T(8,128)(2,1)S(1)} async-done(((bf16[4,56,1536]{2,1,0:T(8,128)(2,1)}), bf16[4,56,1536]{2,1,0:T(8,128)(2,1)S(1)}, u32[]{:S(2)}, u32[]{:S(2)}) %all-to-all-start.2) | async-done | bytes 688160 | tf_op jit(solution)/shard_map/all_to_all | solution.py:169
  88.6 1.1 shard_map.68
  89.8 7.7 %collective-permute-start.10 = (bf16[224,768]{1,0:T(8,128)(2,1)S(1)}, bf16[224,768]{1,0:T(8,128)(2,1)}, u32[]{:S(2)}, u32[]{:S(2)}) collective-permute-start(bf16[224,768]{1,0:T(8,128)(2,1)S(1)} %get-tuple-element.14), channel_id=1, source_target_pairs={{0,64},{64,0},{128,192},{192,128},{256,320},{320,256},{384,448},{4... | collective-permute-start | bytes 1032200 | tf_op jit(solution)/shard_map/ppermute | solution.py:119
  97.5 4.3 %collective-permute-start.6 = (bf16[56,1536]{1,0:T(8,128)(2,1)S(1)}, bf16[56,1536]{1,0:T(8,128)(2,1)S(1)}, u32[]{:S(2)}, u32[]{:S(2)}) collective-permute-start(bf16[56,1536]{1,0:T(8,128)(2,1)S(1)} %get-tuple-element.23), channel_id=1, source_target_pairs={{0,256},{1,257},{2,258},{3,259},{4,260},{5,261},{6,262},{7,263},{1... | collective-permute-start | bytes 516104 | tf_op jit(solution)/shard_map/ppermute | solution.py:107
  101.9 3.7 %collective-permute-start.8 = (bf16[56,1536]{1,0:T(8,128)(2,1)S(1)}, bf16[56,1536]{1,0:T(8,128)(2,1)S(1)}, u32[]{:S(2)}, u32[]{:S(2)}) collective-permute-start(bf16[56,1536]{1,0:T(8,128)(2,1)S(1)} %get-tuple-element.24), channel_id=1, source_target_pairs={{0,128},{1,129},{2,130},{3,131},{4,132},{5,133},{6,134},{7,135},{1... | collective-permute-start | bytes 516104 | tf_op jit(solution)/shard_map/ppermute | solution.py:107
  105.6 2.8 %collective-permute-start.7 = (bf16[56,1536]{1,0:T(8,128)(2,1)S(1)}, bf16[56,1536]{1,0:T(8,128)(2,1)S(1)}, u32[]{:S(2)}, u32[]{:S(2)}) collective-permute-start(bf16[56,1536]{1,0:T(8,128)(2,1)S(1)} %get-tuple-element.25), channel_id=1, source_target_pairs={{0,384},{1,385},{2,386},{3,387},{4,388},{5,389},{6,390},{7,391},{1... | collective-permute-start | bytes 516104 | tf_op jit(solution)/shard_map/ppermute | solution.py:107
  109.2 2.8 %collective-permute-done.7 = bf16[56,1536]{1,0:T(8,128)(2,1)S(1)} collective-permute-done((bf16[56,1536]{1,0:T(8,128)(2,1)S(1)}, bf16[56,1536]{1,0:T(8,128)(2,1)S(1)}, u32[]{:S(2)}, u32[]{:S(2)}) %collective-permute-start.7) | collective-permute-done | bytes 172064 | tf_op jit(solution)/shard_map/ppermute | solution.py:107
  112.8 3.9 %all-to-all-start.3 = ((bf16[8,7,1536]{2,1,0:T(8,128)(2,1)}), bf16[8,7,1536]{2,1,0:T(8,128)(2,1)S(1)}, u32[]{:S(2)}, u32[]{:S(2)}) async-start(bf16[8,7,1536]{2,1,0:T(8,128)(2,1)} %reshape.23), calls=%async_computation.3 | async-start | bytes 393216 | tf_op jit(solution)/shard_map/all_to_all | solution.py:190
  116.8 1.5 %slice_bitcast_fusion = (bf16[224,1536]{1,0:T(8,128)(2,1)S(1)}, bf16[224,1536]{1,0:T(8,128)(2,1)S(1)}) fusion(bf16[2,224,1536]{2,1,0:T(8,128)(2,1)} %collective-permute-done.9), kind=kLoop, calls=%fused_computation.10 | loop fusion | bytes 2752512 | tf_op jit(solution)/shard_map/squeeze | solution.py:196
  118.3 1.0 fusion.24
  119.4 1.8 %convolution_convert_fusion = bf16[384,1536]{1,0:T(8,128)(2,1)} fusion(bf16[224,1536]{1,0:T(8,128)(2,1)S(1)} %get-tuple-element.19, bf16[224,1536]{1,0:T(8,128)(2,1)S(1)} %copy-done.3, bf16[224,384]{1,0:T(8,128)(2,1)S(1)} %get-tuple-element.28, bf16[224,384]{1,0:T(8,128)(2,1)S(1)} %copy-done.5), kind=kOutput, calls=%fused_computation | convolution fusion | flops 532512768 | bytes 2899968 | tf_op jit(solution)/shard_map/dot_general | solution.py:28
  121.2 2.0 %convolution_convert_fusion.1 = bf16[1536,384]{1,0:T(8,128)(2,1)} fusion(bf16[224,1536]{1,0:T(8,128)(2,1)S(1)} %get-tuple-element.20, bf16[224,1536]{1,0:T(8,128)(2,1)S(1)} %copy-done.2, bf16[224,384]{1,0:T(8,128)(2,1)S(1)} %get-tuple-element.29, bf16[224,384]{1,0:T(8,128)(2,1)S(1)} %copy-done.4), kind=kOutput, calls=%fused_computation.1 | convolution fusion | flops 532512768 | bytes 2899968 | tf_op jit(solution)/shard_map/dot_general | solution.py:28
  123.2 4.3 %all-to-all-done.3 = bf16[8,7,1536]{2,1,0:T(8,128)(2,1)S(1)} async-done(((bf16[8,7,1536]{2,1,0:T(8,128)(2,1)}), bf16[8,7,1536]{2,1,0:T(8,128)(2,1)S(1)}, u32[]{:S(2)}, u32[]{:S(2)}) %all-to-all-start.3) | async-done | bytes 172064 | tf_op jit(solution)/shard_map/all_to_all | solution.py:190
  (35 shorter events, 3.0 us)
Async XLA Ops:
  2.2 26.4 %all-to-all-start = ((bf16[8,14,1536]{2,1,0:T(8,128)(2,1)}), bf16[8,14,1536]{2,1,0:T(8,128)(2,1)S(1)}, u32[]{:S(2)}, u32[]{:S(2)}) async-start(bf16[8,14,1536]{2,1,0:T(8,128)(2,1)} %broadcast_in_dim.4), calls=%async_computation | async-start | bytes 786432 | tf_op jit(solution)/shard_map/all_to_all | solution.py:126
  16.1 32.4 %collective-permute-start.4 = (bf16[384,1536]{1,0:T(8,128)(2,1)}, bf16[384,1536]{1,0:T(8,128)(2,1)S(1)}, u32[]{:S(2)}, u32[]{:S(2)}) collective-permute-start(bf16[384,1536]{1,0:T(8,128)(2,1)} %out0.1), channel_id=1, source_target_pairs={{0,64},{64,0},{128,192},{192,128},{256,320},{320,256},{384,448},{4... | collective-permute-start | bytes 3538952 | tf_op jit(solution)/shard_map/ppermute | solution.py:119
  18.0 30.5 %collective-permute-start.3 = (bf16[1536,384]{1,0:T(8,128)(2,1)}, bf16[1536,384]{1,0:T(8,128)(2,1)S(1)}, u32[]{:S(2)}, u32[]{:S(2)}) collective-permute-start(bf16[1536,384]{1,0:T(8,128)(2,1)} %in0.3), channel_id=1, source_target_pairs={{0,64},{64,0},{128,192},{192,128},{256,320},{320,256},{384,448},{4... | collective-permute-start | bytes 3538952 | tf_op jit(solution)/shard_map/ppermute | solution.py:119
  28.8 19.6 %copy-start = (bf16[1536,384]{1,0:T(8,128)(2,1)S(1)}, bf16[1536,384]{1,0:T(8,128)(2,1)}, u32[]{:S(2)}) copy-start(bf16[1536,384]{1,0:T(8,128)(2,1)} %in0.3) | copy-start | bytes 3538948
  28.8 19.6 %copy-start.1 = (bf16[384,1536]{1,0:T(8,128)(2,1)S(1)}, bf16[384,1536]{1,0:T(8,128)(2,1)}, u32[]{:S(2)}) copy-start(bf16[384,1536]{1,0:T(8,128)(2,1)} %out0.1) | copy-start | bytes 3538948
  28.8 9.6 %collective-permute-start.2 = (bf16[56,3072]{1,0:T(8,128)(2,1)S(1)}, bf16[56,3072]{1,0:T(8,128)(2,1)S(1)}, u32[]{:S(2)}, u32[]{:S(2)}) collective-permute-start(bf16[56,3072]{1,0:T(8,128)(2,1)S(1)} %constant_dynamic-update-slice_fusion), channel_id=1, source_target_pairs={{384,0},{385,1},{386,2},{387,3},{388,4},{389,5},{390,6},{391,7},{2... | collective-permute-start | bytes 1032200 | tf_op jit(solution)/shard_map/ppermute | solution.py:104
  31.7 11.5 %collective-permute-start.1 = (bf16[56,3072]{1,0:T(8,128)(2,1)S(1)}, bf16[56,3072]{1,0:T(8,128)(2,1)S(1)}, u32[]{:S(2)}, u32[]{:S(2)}) collective-permute-start(bf16[56,3072]{1,0:T(8,128)(2,1)S(1)} %constant_dynamic-update-slice_fusion), channel_id=1, source_target_pairs={{256,0},{257,1},{258,2},{259,3},{260,4},{261,5},{262,6},{263,7},{3... | collective-permute-start | bytes 1032200 | tf_op jit(solution)/shard_map/ppermute | solution.py:104
  34.3 14.0 %collective-permute-start = (bf16[56,3072]{1,0:T(8,128)(2,1)S(1)}, bf16[56,3072]{1,0:T(8,128)(2,1)S(1)}, u32[]{:S(2)}, u32[]{:S(2)}) collective-permute-start(bf16[56,3072]{1,0:T(8,128)(2,1)S(1)} %constant_dynamic-update-slice_fusion), channel_id=1, source_target_pairs={{128,0},{129,1},{130,2},{131,3},{132,4},{133,5},{134,6},{135,7},{0... | collective-permute-start | bytes 1032200 | tf_op jit(solution)/shard_map/ppermute | solution.py:104
  63.0 13.3 %collective-permute-start.5 = (bf16[56,1536]{1,0:T(8,128)(2,1)S(1)}, bf16[56,1536]{1,0:T(8,128)(2,1)S(1)}, u32[]{:S(2)}, u32[]{:S(2)}) collective-permute-start(bf16[56,1536]{1,0:T(8,128)(2,1)S(1)} %get-tuple-element.15), channel_id=1, source_target_pairs={{0,8},{8,0},{16,24},{24,16},{32,40},{40,32},{48,56},{56,48},{1,9},... | collective-permute-start | bytes 516104 | tf_op jit(solution)/shard_map/ppermute | solution.py:164
  67.4 49.4 %collective-permute-start.9 = (bf16[2,224,1536]{2,1,0:T(8,128)(2,1)}, bf16[2,224,1536]{2,1,0:T(8,128)(2,1)}, u32[]{:S(2)}, u32[]{:S(2)}) collective-permute-start(bf16[2,224,1536]{2,1,0:T(8,128)(2,1)} %get-tuple-element.13), channel_id=1, source_target_pairs={{0,64},{64,0},{128,192},{192,128},{256,320},{320,256},{384,448},{4... | collective-permute-start | bytes 4128776 | tf_op jit(solution)/shard_map/ppermute | solution.py:119
  77.4 11.3 %all-to-all-start.2 = ((bf16[4,56,1536]{2,1,0:T(8,128)(2,1)}), bf16[4,56,1536]{2,1,0:T(8,128)(2,1)S(1)}, u32[]{:S(2)}, u32[]{:S(2)}) async-start(bf16[4,56,1536]{2,1,0:T(8,128)(2,1)} %broadcast_in_dim.5), calls=%async_computation.2 | async-start | bytes 1376256 | tf_op jit(solution)/shard_map/all_to_all | solution.py:169
  89.8 28.5 %collective-permute-start.10 = (bf16[224,768]{1,0:T(8,128)(2,1)S(1)}, bf16[224,768]{1,0:T(8,128)(2,1)}, u32[]{:S(2)}, u32[]{:S(2)}) collective-permute-start(bf16[224,768]{1,0:T(8,128)(2,1)S(1)} %get-tuple-element.14), channel_id=1, source_target_pairs={{0,64},{64,0},{128,192},{192,128},{256,320},{320,256},{384,448},{4... | collective-permute-start | bytes 1032200 | tf_op jit(solution)/shard_map/ppermute | solution.py:119
  97.5 11.6 %collective-permute-start.6 = (bf16[56,1536]{1,0:T(8,128)(2,1)S(1)}, bf16[56,1536]{1,0:T(8,128)(2,1)S(1)}, u32[]{:S(2)}, u32[]{:S(2)}) collective-permute-start(bf16[56,1536]{1,0:T(8,128)(2,1)S(1)} %get-tuple-element.23), channel_id=1, source_target_pairs={{0,256},{1,257},{2,258},{3,259},{4,260},{5,261},{6,262},{7,263},{1... | collective-permute-start | bytes 516104 | tf_op jit(solution)/shard_map/ppermute | solution.py:107
  101.9 7.4 %collective-permute-start.8 = (bf16[56,1536]{1,0:T(8,128)(2,1)S(1)}, bf16[56,1536]{1,0:T(8,128)(2,1)S(1)}, u32[]{:S(2)}, u32[]{:S(2)}) collective-permute-start(bf16[56,1536]{1,0:T(8,128)(2,1)S(1)} %get-tuple-element.24), channel_id=1, source_target_pairs={{0,128},{1,129},{2,130},{3,131},{4,132},{5,133},{6,134},{7,135},{1... | collective-permute-start | bytes 516104 | tf_op jit(solution)/shard_map/ppermute | solution.py:107
  105.6 6.4 %collective-permute-start.7 = (bf16[56,1536]{1,0:T(8,128)(2,1)S(1)}, bf16[56,1536]{1,0:T(8,128)(2,1)S(1)}, u32[]{:S(2)}, u32[]{:S(2)}) collective-permute-start(bf16[56,1536]{1,0:T(8,128)(2,1)S(1)} %get-tuple-element.25), channel_id=1, source_target_pairs={{0,384},{1,385},{2,386},{3,387},{4,388},{5,389},{6,390},{7,391},{1... | collective-permute-start | bytes 516104 | tf_op jit(solution)/shard_map/ppermute | solution.py:107
  112.8 14.8 %all-to-all-start.3 = ((bf16[8,7,1536]{2,1,0:T(8,128)(2,1)}), bf16[8,7,1536]{2,1,0:T(8,128)(2,1)S(1)}, u32[]{:S(2)}, u32[]{:S(2)}) async-start(bf16[8,7,1536]{2,1,0:T(8,128)(2,1)} %reshape.23), calls=%async_computation.3 | async-start | bytes 393216 | tf_op jit(solution)/shard_map/all_to_all | solution.py:190
  116.8 2.6 %copy-start.3 = (bf16[224,1536]{1,0:T(8,128)(2,1)S(1)}, bf16[224,1536]{1,0:T(8,128)(2,1)}, u32[]{:S(2)}) copy-start(bf16[224,1536]{1,0:T(8,128)(2,1)} %get-tuple-element.17) | copy-start | bytes 2064388
  116.8 2.6 %copy-start.5 = (bf16[224,384]{1,0:T(8,128)(2,1)S(1)}, bf16[224,384]{1,0:T(8,128)(2,1)}, u32[]{:S(2)}) copy-start(bf16[224,384]{1,0:T(8,128)(2,1)} %get-tuple-element.21) | copy-start | bytes 516100
  119.3 1.8 %copy-start.2 = (bf16[224,1536]{1,0:T(8,128)(2,1)S(1)}, bf16[224,1536]{1,0:T(8,128)(2,1)}, u32[]{:S(2)}) copy-start(bf16[224,1536]{1,0:T(8,128)(2,1)} %get-tuple-element.18) | copy-start | bytes 2064388
  119.4 1.8 %copy-start.4 = (bf16[224,384]{1,0:T(8,128)(2,1)S(1)}, bf16[224,384]{1,0:T(8,128)(2,1)}, u32[]{:S(2)}) copy-start(bf16[224,384]{1,0:T(8,128)(2,1)} %get-tuple-element.22) | copy-start | bytes 516100
